TPU v7x, 256 devices: a whole 4x4x8 slice. The times are simulated.
256 devices in a mesh: dp: 8 (over x, core), owner: 32 (over z, y).
Axes of the slice: x: 4, y: 4, z: 8, core: 2. Of those that a mesh axis runs over, the one named last changes fastest.
Arguments:
- grads: bfloat16 [8, 224, 512, 512], P('dp', 'owner'), may hold values from -1.5 to 1.5
- plan: int32 [224], replicated, may hold values from 0 to 31, as said below
- left_stat: float32 [32, 13, 512, 512], P('owner', None, 'dp'), as said below
- right_stat: float32 [32, 13, 512, 512], P('owner', None, 'dp'), as said below
- left_root: bfloat16 [32, 13, 512, 512], P('owner', None, 'dp'), as said below
- right_root: bfloat16 [32, 13, 512, 512], P('owner', None, 'dp'), as said below
Outputs:
- left_new: float32 [32, 13, 512, 512], P('owner', None, 'dp')
- right_new: float32 [32, 13, 512, 512], P('owner', None, 'dp')
- update: float32 [224, 512, 512], P('owner', 'dp')
Inputs may be any that keep to these rules, and one draw needn't show every extreme that they name: `plan`: the 7 blocks i * 7 to i * 7 + 6 go to 7 different owners. Every owner receives between 1 and 13 blocks, and some owner receives exactly 13. `left_stat`: each slot's matrix is symmetric. `right_stat`: each slot's matrix is symmetric. `left_root`: each slot's matrix is symmetric. `right_root`: each slot's matrix is symmetric.
All inputs are finite; a program needn't handle non-finite values.
Results may differ from a plain program's by a relative error of at most 0.0003.
Values may be sent and summed in bfloat16 or wider, within the bound.
A program may use at most 128 MiB of HBM per device.

v0:
```python
import jax
import jax.numpy as jnp
from jax import lax
from jax.sharding import PartitionSpec as P

highest = lax.Precision.HIGHEST
stat_decay = 0.95
fresh_share = 0.05


def local(grads, plan, left_stat, right_stat, left_root, right_root):
    dp_count = lax.axis_size("dp")
    owner_count = lax.axis_size("owner")
    dp_place = lax.axis_index("dp")
    owner_place = lax.axis_index("owner")
    blocks = grads.shape[1]
    block_order = grads.shape[3]
    stripe = block_order // dp_count
    slot_count = left_stat.shape[1]
    partial_sum = lax.psum_scatter(
        grads[0].astype(jnp.float32), "dp", scatter_dimension=1, tiled=True
    )
    plan_table = plan.reshape(owner_count, blocks)
    my_owners = lax.dynamic_index_in_dim(plan_table, owner_place, 0, keepdims=False)
    owner_ids = jnp.arange(owner_count, dtype=jnp.int32)
    outward = (owner_ids[:, None] == my_owners[None, :]).astype(jnp.float32)
    holding = jnp.sum((plan_table == owner_place).astype(jnp.int32), axis=1)
    standing = jnp.cumsum(holding) - 1
    slot_ids = jnp.arange(slot_count, dtype=jnp.int32)
    inward = ((slot_ids[:, None] == standing[None, :]) & (holding[None, :] > 0)).astype(jnp.float32)
    column_start = dp_place * stripe

    def statistics(own_rows, left_rows):

        def fold_step(state_now, shard_rows, first_row):
            facing = jnp.einsum("kac,kqc->kaq", own_rows, shard_rows, precision=highest)
            own_cols = lax.dynamic_slice_in_dim(shard_rows, column_start, stripe, 2)
            right_part = jnp.einsum("kqa,kqc->kac", own_cols, shard_rows, precision=highest)
            projected = jnp.einsum("kaq,kqc->kac", left_rows, shard_rows, precision=highest)
            return (facing, right_part, projected)

        zero_rows = jnp.zeros(own_rows.shape, jnp.float32)
        return (fold_step, (zero_rows, zero_rows, zero_rows))

    payload = jnp.stack((left_root[0], right_root[0]), axis=1)
    leaving = jnp.einsum(
        "ks,kxac->sxac", inward.astype(jnp.bfloat16), payload, preferred_element_type=jnp.float32
    ).astype(jnp.bfloat16)
    arriving = lax.all_to_all(leaving, "owner", split_axis=0, concat_axis=0, tiled=True)
    chosen = jnp.einsum(
        "oj,oxac->jxac", outward.astype(jnp.bfloat16), arriving, preferred_element_type=jnp.float32
    )
    left_rows = chosen[:, 0]
    right_rows = chosen[:, 1].astype(jnp.bfloat16)
    fold_step, start_value = statistics(partial_sum, left_rows)
    left_part, right_part, projected = fold_step(
        start_value, lax.all_gather(partial_sum, "dp", axis=1, tiled=True), jnp.int32(0)
    )
    term_pair = jnp.stack((left_part, right_part), axis=1)
    sending = jnp.einsum("oj,jxac->oxac", outward, term_pair, precision=highest)
    received = lax.all_to_all(sending, "owner", split_axis=0, concat_axis=0, tiled=True)
    slot_terms = jnp.einsum("ks,sxac->kxac", inward, received, precision=highest)
    left_term = slot_terms[:, 0]
    right_term = slot_terms[:, 1]
    shard_rows = lax.all_gather(right_rows, "dp", axis=1, tiled=True)
    update = jnp.einsum(
        "kaq,kqc->kac", projected, shard_rows.astype(jnp.float32), precision=highest
    )
    left_new = stat_decay * left_stat[0] + fresh_share * left_term
    right_new = stat_decay * right_stat[0] + fresh_share * right_term
    return (left_new[None], right_new[None], update)


def solution(mesh):
    return jax.shard_map(
        local,
        mesh=mesh,
        in_specs=(
            P("dp", "owner", None, None),
            P(),
            P("owner", None, "dp", None),
            P("owner", None, "dp", None),
            P("owner", None, "dp", None),
            P("owner", None, "dp", None),
        ),
        out_specs=(
            P("owner", None, "dp", None),
            P("owner", None, "dp", None),
            P("owner", "dp", None),
        ),
        check_vma=False,
    )
```

profile of v0, /device:TPU:122, one launch (start us, length us, event | category | flops | bytes accessed | tf_op | source)
XLA Modules:
  0.0 410.4 jit_solution(14226632484095687047)
XLA Ops:
  7.2 6.0 %bitcast_convert_fusion = f32[7,512,512]{2,1,0:T(8,128)} fusion(bf16[1,7,512,512]{3,2,1,0:T(8,128)(2,1)} %param.6), kind=kLoop, calls=%fused_computation.4 | loop fusion | flops 1835008 | bytes 11010048 | tf_op jit(solution)/shard_map/convert_element_type | solution.py:21
  13.3 49.5 %reduce-scatter.2.cloned.1.call-done = f32[7,64,512]{2,1,0:T(8,128)} async-done(((f32[7,512,512]{2,1,0:T(8,128)}), f32[7,64,512]{2,1,0:T(8,128)}) %reduce-scatter.2.cloned.1.call-update) | async-done | bytes 917520 | tf_op jit(solution)/shard_map/reduce_scatter | solution.py:20
  62.8 0.1 reshape.67
  62.9 0.1 convert_reduce_fusion
  63.1 0.1 copy.24
  63.1 0.1 reduce-window.8
  63.2 0.1 add_reduce_fusion
  63.4 1.0 copy_bitcast_fusion
  64.3 1.3 convolution_convert_fusion
  65.6 4.4 %copy.32 = bf16[32,2,64,512]{3,2,1,0:T(8,128)(2,1)} copy(bf16[32,2,64,512]{3,0,2,1:T(8,128)(2,1)S(1)} %convolution_convert_fusion) | data formatting | bytes 8388608 | tf_op jit(solution)/shard_map/convert_element_type | solution.py:48
  70.0 9.9 %all-to-all-start.1 = ((bf16[32,2,64,512]{3,2,1,0:T(8,128)(2,1)}), bf16[32,2,64,512]{3,2,1,0:T(8,128)(2,1)}, u32[]{:S(2)}, u32[]{:S(2)}) async-start(bf16[32,2,64,512]{3,2,1,0:T(8,128)(2,1)} %copy.32), calls=%async_computation.2 | async-start | bytes 8388608 | tf_op jit(solution)/shard_map/all_to_all | solution.py:49
  79.9 33.5 %all-gather.4.cloned.1.call-done = f32[7,512,512]{2,1,0:T(8,128)} async-done(((f32[7,64,512]{2,1,0:T(8,128)}), f32[7,512,512]{2,1,0:T(8,128)}) %all-gather.4.cloned.1.call-update) | async-done | bytes 7340048 | tf_op jit(solution)/shard_map/all_gather | solution.py:57
  113.5 10.7 %fusion.17 = f32[7,1,64,512]{3,2,0,1:T(8,128)S(1)} fusion(f32[7,512,512]{2,1,0:T(8,128)} %all-gather.4.cloned.1.call-done, s32[]{:T(128)S(6)} %select_n.8), kind=kOutput, calls=%fused_computation.24 | convolution fusion | flops 1409286144 | bytes 10092548 | tf_op jit(solution)/shard_map/kqa,kqc->kac/dot_general | solution.py:38
  124.2 7.2 %convolution_bitcast_fusion = f32[7,1,64,512]{3,2,0,1:T(8,128)S(1)} fusion(f32[7,64,512]{2,1,0:T(8,128)S(1)} %copy-done.1, f32[7,512,512]{2,1,0:T(8,128)S(1)} %copy-done), kind=kOutput, calls=%fused_computation.25 | convolution fusion | flops 1409286144 | bytes 9175040 | tf_op jit(solution)/shard_map/kac,kqc->kaq/dot_general | solution.py:36
  131.4 0.2 pad_maximum_fusion
  131.6 4.3 %fusion.13 = f32[32,2,64,512]{3,0,2,1:T(8,128)S(1)} fusion(f32[7,2,64,512]{3,2,0,1:T(8,128)S(1)} %pad_maximum_fusion, s32[7]{0:T(128)S(1)} %dynamic-slice_bitcast_fusion), kind=kOutput, calls=%fused_computation.18 | convolution fusion | flops 176160992 | bytes 10223644 | tf_op jit(solution)/shard_map/oj,jxac->oxac/dot_general | solution.py:60
  135.9 8.3 %copy.27 = f32[32,2,64,512]{3,2,1,0:T(8,128)} copy(f32[32,2,64,512]{3,0,2,1:T(8,128)S(1)} %fusion.13) | data formatting | bytes 16777216 | tf_op jit(solution)/shard_map/oj,jxac->oxac/dot_general | solution.py:60
  144.2 34.1 %all-to-all-done.1 = bf16[32,2,64,512]{3,2,1,0:T(8,128)(2,1)} async-done(((bf16[32,2,64,512]{3,2,1,0:T(8,128)(2,1)}), bf16[32,2,64,512]{3,2,1,0:T(8,128)(2,1)}, u32[]{:S(2)}, u32[]{:S(2)}) %all-to-all-start.1) | async-done | bytes 4194336 | tf_op jit(solution)/shard_map/all_to_all | solution.py:49
  178.3 7.9 %all-to-all-start = ((f32[32,2,64,512]{3,2,1,0:T(8,128)}), f32[32,2,64,512]{3,2,1,0:T(8,128)}, u32[]{:S(2)}, u32[]{:S(2)}) async-start(f32[32,2,64,512]{3,2,1,0:T(8,128)} %copy.27), calls=%async_computation.1 | async-start | bytes 16777216 | tf_op jit(solution)/shard_map/all_to_all | solution.py:61
  186.2 0.0 all-gather.6.cloned.1.call-start
  186.3 4.6 %fusion.2 = f32[7,2,64,512]{3,0,2,1:T(8,128)S(1)} fusion(bf16[32,2,64,512]{3,2,1,0:T(8,128)(2,1)} %all-to-all-done.1, s32[7]{0:T(128)S(1)} %dynamic-slice_bitcast_fusion), kind=kOutput, calls=%fused_computation.2 | convolution fusion | flops 29360800 | bytes 6029340 | tf_op jit(solution)/shard_map/oj,oxac->jxac/dot_general | solution.py:50
  190.8 0.1 slice.33
  190.9 0.9 copy.35
  191.9 0.1 slice_bitcast_fusion
  191.9 7.7 %fusion.20 = f32[7,64,512]{2,1,0:T(8,128)S(1)} fusion(f32[7,512,512]{2,1,0:T(8,128)} %all-gather.4.cloned.1.call-done, f32[7,64,512]{2,0,1:T(8,128)S(1)} %slice_bitcast_fusion), kind=kOutput, calls=%fused_computation.30 | convolution fusion | flops 1409286144 | bytes 9175040 | tf_op jit(solution)/shard_map/kaq,kqc->kac/dot_general | solution.py:39
  199.7 23.8 %all-gather.6.cloned.1.call-done = bf16[7,1,512,512]{3,2,1,0:T(8,128)(2,1)} async-done(((bf16[7,1,64,512]{3,2,1,0:T(8,128)(2,1)}), bf16[7,1,512,512]{3,2,1,0:T(8,128)(2,1)}) %all-gather.6.cloned.1.call-update) | async-done | bytes 3670032 | tf_op jit(solution)/shard_map/all_gather | solution.py:65
  223.5 5.0 %fusion.4 = f32[7,64,512]{2,1,0:T(8,128)} fusion(f32[7,64,512]{2,1,0:T(8,128)S(1)} %fusion.20, bf16[7,1,512,512]{3,2,1,0:T(8,128)(2,1)} %all-gather.6.cloned.1.call-done), kind=kOutput, calls=%fused_computation.5 | convolution fusion | flops 1409286144 | bytes 5505024 | tf_op jit(solution)/shard_map/kaq,kqc->kac/dot_general | solution.py:66
  228.4 153.6 %all-to-all-done = f32[32,2,64,512]{3,2,1,0:T(8,128)} async-done(((f32[32,2,64,512]{3,2,1,0:T(8,128)}), f32[32,2,64,512]{3,2,1,0:T(8,128)}, u32[]{:S(2)}, u32[]{:S(2)}) %all-to-all-start) | async-done | bytes 8388640 | tf_op jit(solution)/shard_map/all_to_all | solution.py:61
  382.1 14.1 %fusion = f32[13,2,64,512]{3,0,2,1:T(8,128)S(1)} fusion(f32[32,2,64,512]{3,2,1,0:T(8,128)} %all-to-all-done, s32[32]{0:T(128)S(1)} %add_reduce_fusion, pred[32]{0:T(512)(128)(4,1)S(1)} %broadcast_compare_fusion), kind=kOutput, calls=%fused_computation | convolution fusion | flops 327156544 | bytes 11796640 | tf_op jit(solution)/shard_map/ks,sxac->kxac/dot_general | solution.py:62
  396.2 2.8 fusion.7
  399.0 2.2 copy.37
  401.2 2.2 copy.36
  (21 shorter events, 0.2 us)
Async XLA Ops:
  7.2 55.6 %reduce-scatter.2.cloned.1.call-start = ((), (), s32[]{:S(2)}) async-start(), calls=%async_computation.3 | async-start | bytes 8257536 | tf_op jit(solution)/shard_map/reduce_scatter | solution.py:20
  13.2 49.6 %copy-start.6 = (s32[224]{0:T(256)S(1)}, s32[224]{0:T(256)}, u32[]{:S(2)}) copy-start(s32[224]{0:T(256)} %param.7) | copy-start | bytes 2692
  13.2 50.1 %copy-start.4 = (bf16[1,13,64,512]{3,2,1,0:T(8,128)(2,1)S(1)}, bf16[1,13,64,512]{3,2,1,0:T(8,128)(2,1)}, u32[]{:S(2)}) copy-start(bf16[1,13,64,512]{3,2,1,0:T(8,128)(2,1)} %param.11) | copy-start | bytes 2555908
  13.2 50.1 %copy-start.5 = (bf16[1,13,64,512]{3,2,1,0:T(8,128)(2,1)S(1)}, bf16[1,13,64,512]{3,2,1,0:T(8,128)(2,1)}, u32[]{:S(2)}) copy-start(bf16[1,13,64,512]{3,2,1,0:T(8,128)(2,1)} %param.10) | copy-start | bytes 2555908
  13.2 100.2 %all-gather.4.cloned.1.call-start = ((), (), s32[]{:S(2)}) async-start(), calls=%async_computation.4 | async-start | bytes 8257536 | tf_op jit(solution)/shard_map/all_gather | solution.py:57
  70.0 108.4 %all-to-all-start.1 = ((bf16[32,2,64,512]{3,2,1,0:T(8,128)(2,1)}), bf16[32,2,64,512]{3,2,1,0:T(8,128)(2,1)}, u32[]{:S(2)}, u32[]{:S(2)}) async-start(bf16[32,2,64,512]{3,2,1,0:T(8,128)(2,1)} %copy.32), calls=%async_computation.2 | async-start | bytes 8388608 | tf_op jit(solution)/shard_map/all_to_all | solution.py:49
  79.9 44.2 %copy-start.1 = (f32[7,64,512]{2,1,0:T(8,128)S(1)}, f32[7,64,512]{2,1,0:T(8,128)}, u32[]{:S(2)}) copy-start(f32[7,64,512]{2,1,0:T(8,128)} %reduce-scatter.2.cloned.1.call-done) | copy-start | bytes 2752516
  113.5 10.7 %copy-start = (f32[7,512,512]{2,1,0:T(8,128)S(1)}, f32[7,512,512]{2,1,0:T(8,128)}, u32[]{:S(2)}) copy-start(f32[7,512,512]{2,1,0:T(8,128)} %all-gather.4.cloned.1.call-done) | copy-start | bytes 22020100
  178.3 203.7 %all-to-all-start = ((f32[32,2,64,512]{3,2,1,0:T(8,128)}), f32[32,2,64,512]{3,2,1,0:T(8,128)}, u32[]{:S(2)}, u32[]{:S(2)}) async-start(f32[32,2,64,512]{3,2,1,0:T(8,128)} %copy.27), calls=%async_computation.1 | async-start | bytes 16777216 | tf_op jit(solution)/shard_map/all_to_all | solution.py:61
  186.2 37.2 %all-gather.6.cloned.1.call-start = ((), (), s32[]{:S(2)}) async-start(), calls=%async_computation.5 | async-start | bytes 4128768 | tf_op jit(solution)/shard_map/all_gather | solution.py:65
  228.4 167.7 %copy-start.2 = (f32[1,13,64,512]{3,2,1,0:T(8,128)S(1)}, f32[1,13,64,512]{3,2,1,0:T(8,128)}, u32[]{:S(2)}) copy-start(f32[1,13,64,512]{3,2,1,0:T(8,128)} %param.9) | copy-start | bytes 5111812
  228.4 167.7 %copy-start.3 = (f32[1,13,64,512]{3,2,1,0:T(8,128)S(1)}, f32[1,13,64,512]{3,2,1,0:T(8,128)}, u32[]{:S(2)}) copy-start(f32[1,13,64,512]{3,2,1,0:T(8,128)} %param.8) | copy-start | bytes 5111812
Sparse Core Ops, SparseCore 0:
  13.4 49.4 reduce-scatter.1
  64.6 48.7 all-gather.3
  192.0 31.4 all-gather.5
where the time goes:
time: 418 us; the launch traced here: 410 us
  waiting for transfers between devices  295 us (71%)
  matrix products  54.9 us (13%)
  local copies, waits for them, and re-layouts  19.2 us (5%)
  starting transfers between devices  17.9 us (4%)
  between operations  14.4 us (3%)
  other arithmetic  9.32 us (2%)
    all_to_all x1, waiting for transfers between devices, local(): lax.all_to_all(sending, 'owner', split_axis=0, concat_axis=0, tiled=True)  154 us
    reduce_scatter x1, waiting for transfers between devices, local(): lax.psum_scatter(grads[0].astype(jnp.float32), 'dp', scatter_dimension=1,...  49.5 us
    all_to_all x1, waiting for transfers between devices, local(): lax.all_to_all(leaving, 'owner', split_axis=0, concat_axis=0, tiled=True)  34.1 us
    all_gather x1, waiting for transfers between devices, local(): lax.all_gather(partial_sum, 'dp', axis=1, tiled=True)  33.5 us
    all_gather x1, waiting for transfers between devices, local(): shard_rows = lax.all_gather(right_rows, 'dp', axis=1, tiled=True)  23.8 us
    dot_general x1, matrix products, local(): jnp.einsum('ks,sxac->kxac', inward, received, precision=highest)  14.1 us
    dot_general x1, matrix products, fold_step(): jnp.einsum('kqa,kqc->kac', own_cols, shard_rows, precision=highest)  10.7 us
    all_to_all x1, starting transfers between devices, local(): lax.all_to_all(leaving, 'owner', split_axis=0, concat_axis=0, tiled=True)  9.91 us
  transfers between devices with their start and end apart: 5, of which 5 were waited for; matrix products, arithmetic and copies ran while one was open for 14% of the time, Pallas kernels for 0%

commit v1 on v0

v1 whole, which is shorter than its diff:
```python
import functools

import jax
import jax.numpy as jnp
from jax import lax
from jax.experimental import pallas as pl
from jax.experimental.pallas import tpu as pltpu
from jax.sharding import PartitionSpec as P

MESH = pl.DeviceIdType.MESH
f32 = jnp.float32
bf16 = jnp.bfloat16
i16 = jnp.int16
i32 = jnp.int32

stat_decay = 0.95
fresh_share = 0.05

NB = 7
NO = 32
NS = 13
ND = 8
SR = 64
BO = 512
CH = 128
SLOT = 272
UNIT = 912
CUT = 7
LIMIT = 60 * 1024 * 1024


def encode(x):
    m = jnp.maximum(jnp.max(jnp.abs(x), axis=0, keepdims=True), 2.0 ** -100)
    e = jnp.floor(jnp.log2(m) * 256.0) + 1.0
    q = jnp.round(x * (32700.0 * jnp.exp2(e * (-1.0 / 256.0))))
    return q.astype(i32).astype(i16), e


def scale_of(e16):
    return jnp.exp2(e16.astype(i32).astype(f32) * (1.0 / 256.0)) * (1.0 / 32700.0)


def widen(q):
    return q.astype(i32).astype(f32)


def remote(src, dst, send, recv, where):
    return pltpu.make_async_remote_copy(
        src_ref=src, dst_ref=dst, send_sem=send, recv_sem=recv,
        device_id=where, device_id_type=MESH)


def ring_places():
    dp = lax.axis_index("dp")
    x, c = dp // 2, dp % 2
    partner = x * 2 + 1 - c
    right = ((x + 1) % 4) * 2 + c
    left = ((x + 3) % 4) * 2 + c
    across = ((x + 2) % 4) * 2 + c
    return dp, x, c, partner, right, left, across


def greet(barrier, places):
    for place in places:
        pl.semaphore_signal(barrier, inc=1, device_id={"dp": place}, device_id_type=MESH)


def greet_owners(barrier, me):
    def one(k, _):
        pl.semaphore_signal(
            barrier, inc=1, device_id={"owner": (me + k) % NO}, device_id_type=MESH)
        return 0

    lax.fori_loop(1, NO, one, 0)


def sum_kernel(grads, g7, own, par, snd, rcv, psend, precv, lsem, usend, urecv):
    dp, x, c, partner, right, left, across = ring_places()
    barrier = pltpu.get_barrier_semaphore()
    greet(barrier, (partner, right, left))
    pl.semaphore_wait(barrier, 3)
    pair, mine = [], []
    for n, off in enumerate((2, 1, 3, 0)):
        xd = (x + off) % 4
        there = pl.ds(pl.multiple_of((xd * 2 + 1 - c) * SR, SR), SR)
        here = pl.ds(pl.multiple_of((xd * 2 + c) * SR, SR), SR)
        cp = remote(grads.at[:, there, :], par.at[n], psend.at[n], precv.at[n], {"dp": partner})
        cp.start()
        pair.append(cp)
        lc = pltpu.make_async_copy(grads.at[:, here, :], own.at[n], lsem.at[n])
        lc.start()
        mine.append(lc)

    row_id = lax.broadcasted_iota(i32, (16, CH), 0)

    def pair_sum(n, j, k):
        cols = slice(k * CH, k * CH + CH)
        return own[n, j, :, cols].astype(f32) + par[n, j, :, cols].astype(f32)

    def unit_rows(j, kk):
        return pl.ds(pl.multiple_of(j * 128 + kk * SR, SR), SR)

    def received(u, j, kk):
        scales = scale_of(rcv[u, 896:912, :])
        row = jnp.sum(jnp.where(row_id == j * 2 + kk, scales, 0.0), axis=0, keepdims=True)
        return widen(rcv[u, unit_rows(j, kk), :]) * row

    def fill(u, value):
        def block(j, sc):
            for kk in range(2):
                q, e = encode(value(j, kk))
                snd[u, unit_rows(j, kk), :] = q
                sc = jnp.where(row_id == j * 2 + kk, e, sc)
            return sc

        sc = lax.fori_loop(0, NB, block, jnp.zeros((16, CH), f32))
        snd[u, 896:912, :] = sc.astype(i32).astype(i16)

    def ship(u, place):
        cp = remote(snd.at[u], rcv.at[u], usend.at[u], urecv.at[u], {"dp": place})
        cp.start()
        return cp

    def ready(n):
        mine[n].wait()
        pair[n].wait_recv()

    ready(0)
    fill(0, lambda j, kk: pair_sum(0, j, kk))
    c0 = ship(0, right)
    fill(1, lambda j, kk: pair_sum(0, j, 2 + kk))
    c1 = ship(1, left)
    ready(1)
    fill(2, lambda j, kk: pair_sum(1, j, 2 + kk))
    c2 = ship(2, right)
    ready(2)
    fill(3, lambda j, kk: pair_sum(2, j, kk))
    c3 = ship(3, left)
    c0.wait_recv()
    fill(4, lambda j, kk: pair_sum(1, j, kk) + received(0, j, kk))
    c4 = ship(4, right)
    c1.wait_recv()
    fill(5, lambda j, kk: pair_sum(2, j, 2 + kk) + received(1, j, kk))
    c5 = ship(5, left)
    ready(3)
    c2.wait_recv()
    c3.wait_recv()
    c4.wait_recv()
    c5.wait_recv()

    def total(j, _):
        sc = jnp.zeros((16, CH), f32)
        for k in range(4):
            kk = k % 2
            one, two = ((4, 3), (2, 5))[k // 2]
            v = pair_sum(3, j, k) + received(one, j, kk) + received(two, j, kk)
            q, e = encode(v)
            g7[j, k * SR:k * SR + SR, :] = q
            sc = jnp.where(row_id == k, e, sc)
        g7[j, 256:272, :] = sc.astype(i32).astype(i16)
        return 0

    lax.fori_loop(0, NB, total, 0)
    for cp in (c0, c1, c2, c3, c4, c5):
        cp.wait_send()
    for cp in pair:
        cp.wait_send()


def sum_over_dp(grads):
    return pl.pallas_call(
        sum_kernel,
        out_shape=jax.ShapeDtypeStruct((NB, SLOT, CH), i16),
        in_specs=[pl.BlockSpec(memory_space=pl.ANY)],
        out_specs=pl.BlockSpec(memory_space=pltpu.VMEM),
        scratch_shapes=[
            pltpu.VMEM((4, NB, SR, BO), bf16),
            pltpu.VMEM((4, NB, SR, BO), bf16),
            pltpu.VMEM((6, UNIT, CH), i16),
            pltpu.VMEM((6, UNIT, CH), i16),
            pltpu.SemaphoreType.DMA((4,)),
            pltpu.SemaphoreType.DMA((4,)),
            pltpu.SemaphoreType.DMA((4,)),
            pltpu.SemaphoreType.DMA((6,)),
            pltpu.SemaphoreType.DMA((6,)),
        ],
        compiler_params=pltpu.CompilerParams(
            collective_id=0, has_side_effects=True, vmem_limit_bytes=LIMIT),
        name="sum_over_dp",
    )(grads)


class Gather:
    def __init__(self, src, full, send, recv):
        self.src, self.full, self.send, self.recv = src, full, send, recv
        self.sent = []

    def _go(self, n, src, dst, place):
        cp = remote(src, dst, self.send.at[n], self.recv.at[n], {"dp": place})
        cp.start()
        self.sent.append(cp)
        return cp

    def begin(self):
        dp, x, c, partner, right, left, across = ring_places()
        a, b = slice(0, CUT), slice(CUT, NS)
        full, src = self.full, self.src
        self.ra = self._go(0, src.at[a], full.at[dp, a], right)
        self.lb = self._go(1, src.at[b], full.at[dp, b], left)
        self.rb = self._go(2, src.at[b], full.at[dp, b], right)
        self.la = self._go(3, src.at[a], full.at[dp, a], left)
        self.own = self._go(4, src, full.at[dp], partner)

    def finish(self):
        dp, x, c, partner, right, left, across = ring_places()
        a, b = slice(0, CUT), slice(CUT, NS)
        full = self.full
        self.ra.wait_recv()
        fa = self._go(5, full.at[left, a], full.at[left, a], right)
        pa = self._go(6, full.at[left, a], full.at[left, a], partner)
        self.lb.wait_recv()
        fb = self._go(7, full.at[right, b], full.at[right, b], left)
        pb = self._go(8, full.at[right, b], full.at[right, b], partner)
        self.rb.wait_recv()
        pc = self._go(9, full.at[left, b], full.at[left, b], partner)
        self.la.wait_recv()
        pd = self._go(10, full.at[right, a], full.at[right, a], partner)
        fa.wait_recv()
        pe = self._go(11, full.at[across, a], full.at[across, a], partner)
        fb.wait_recv()
        pf = self._go(12, full.at[across, b], full.at[across, b], partner)
        for cp in (self.own, pa, pb, pc, pd, pe, pf):
            cp.wait_recv()

    def end(self):
        for cp in self.sent:
            cp.wait_send()


GATHER_SEMS = 13


def exchange_start(me, fetch, send, recv, ssem, rsem):
    def one(k, _):
        dest = (me + k) % NO
        send[k] = fetch(dest)
        remote(send.at[k], recv.at[me], ssem.at[k], rsem.at[k], {"owner": dest}).start()
        return 0

    lax.fori_loop(1, NO, one, 0)
    recv[me] = fetch(me)


def exchange_wait(me, send, recv, ssem, rsem):
    def one(k, _):
        came = (me + NO - k) % NO
        cp = remote(send.at[k], recv.at[came], ssem.at[k], rsem.at[k], {"owner": came})
        cp.wait_recv()
        cp.wait_send()
        return 0

    lax.fori_loop(1, NO, one, 0)


def out_kernel(block_of, source_of, g7, right_root, slots, rfull,
               send, recv, ssem, rsem, gsend, grecv, lsem):
    me = lax.axis_index("owner")
    dp, x, c, partner, right, left, across = ring_places()
    barrier = pltpu.get_barrier_semaphore()
    greet(barrier, (partner, right, left))
    greet_owners(barrier, me)
    pl.semaphore_wait(barrier, 3 + NO - 1)
    gather = Gather(right_root, rfull, gsend, grecv)
    gather.begin()
    local = pltpu.make_async_copy(right_root, rfull.at[dp], lsem)
    local.start()
    exchange_start(me, lambda dest: g7[block_of[dest]], send, recv, ssem, rsem)
    gather.finish()
    exchange_wait(me, send, recv, ssem, rsem)

    def pick(k, _):
        slots[k] = recv[source_of[k]]
        return 0

    lax.fori_loop(0, NS, pick, 0)
    gather.end()
    local.wait()


def to_owners(block_of, source_of, g7, right_root):
    return pl.pallas_call(
        out_kernel,
        out_shape=(
            jax.ShapeDtypeStruct((NS, SLOT, CH), i16),
            jax.ShapeDtypeStruct((ND, NS, SR, BO), bf16),
        ),
        in_specs=[
            pl.BlockSpec(memory_space=pltpu.SMEM),
            pl.BlockSpec(memory_space=pltpu.SMEM),
            pl.BlockSpec(memory_space=pltpu.VMEM),
            pl.BlockSpec(memory_space=pl.ANY),
        ],
        out_specs=(
            pl.BlockSpec(memory_space=pltpu.VMEM),
            pl.BlockSpec(memory_space=pl.ANY),
        ),
        scratch_shapes=[
            pltpu.VMEM((NO, SLOT, CH), i16),
            pltpu.VMEM((NO, SLOT, CH), i16),
            pltpu.SemaphoreType.DMA((NO,)),
            pltpu.SemaphoreType.DMA((NO,)),
            pltpu.SemaphoreType.DMA((GATHER_SEMS,)),
            pltpu.SemaphoreType.DMA((GATHER_SEMS,)),
            pltpu.SemaphoreType.DMA,
        ],
        compiler_params=pltpu.CompilerParams(
            collective_id=1, has_side_effects=True, vmem_limit_bytes=LIMIT),
        name="to_owners",
    )(block_of, source_of, g7, right_root)


def dot(a, b, dims=((1,), (0,))):
    return lax.dot_general(a, b, (dims, ((), ())), preferred_element_type=f32)


def split(v):
    hi = v.astype(bf16)
    return hi, (v - hi.astype(f32)).astype(bf16)


def back_kernel(slot_of, owner_of, weight, slots, rfull, left_root, left_stat, right_stat,
                left_new, right_new, update,
                codes, high, low, rv, lv, ls, rs, term, usl, send, recv,
                ssem, rsem, gsend, grecv, lsem, osem):
    me = lax.axis_index("owner")
    dp, x, c, partner, right, left, across = ring_places()
    loads = [
        pltpu.make_async_copy(slots, codes.at[dp], lsem.at[0]),
        pltpu.make_async_copy(left_root, lv, lsem.at[1]),
        pltpu.make_async_copy(rfull, rv, lsem.at[2]),
        pltpu.make_async_copy(left_stat, ls, lsem.at[3]),
        pltpu.make_async_copy(right_stat, rs, lsem.at[4]),
    ]
    for cp in loads:
        cp.start()
    barrier = pltpu.get_barrier_semaphore()
    greet(barrier, (partner, right, left))
    greet_owners(barrier, me)
    pl.semaphore_wait(barrier, 3 + NO - 1)
    gather = Gather(slots, codes, gsend, grecv)
    gather.begin()
    gather.finish()
    for cp in loads:
        cp.wait()

    row_id = lax.broadcasted_iota(i32, (16, CH), 0)

    def make_update(k, _):
        for t in range(ND):
            scales = scale_of(codes[t, k, 256:272, :])
            for n in range(4):
                v = widen(codes[t, k, n * SR:n * SR + SR, :]) * scales[n:n + 1, :]
                hi, lo = split(v)
                high[k, t * SR:t * SR + SR, n * CH:n * CH + CH] = hi
                low[k, t * SR:t * SR + SR, n * CH:n * CH + CH] = lo
        lrows = lv[k]
        projected = dot(lrows, high[k]) + dot(lrows, low[k])
        phi, plo = split(projected)
        both = dot(jnp.concatenate((phi, plo), axis=0), rv[:, k].reshape(BO, BO))
        u = both[:SR] + both[SR:]
        sc = jnp.zeros((16, CH), f32)
        for n in range(4):
            q, e = encode(u[:, n * CH:n * CH + CH])
            usl[k, n * SR:n * SR + SR, :] = q
            sc = jnp.where(row_id == n, e, sc)
        usl[k, 256:272, :] = sc.astype(i32).astype(i16)
        return 0

    lax.fori_loop(0, NS, make_update, 0)
    exchange_start(me, lambda dest: usl[slot_of[dest]], send, recv, ssem, rsem)

    rows = pl.ds(pl.multiple_of(dp * SR, SR), SR)
    lanes = pl.ds(pl.multiple_of(x * CH, CH), CH)
    side = pl.ds(pl.multiple_of(c * SR, SR), SR)

    def make_stats(k, _):
        w = weight[k]
        hi, lo = high[k], low[k]
        ohi, olo = high[k, rows, :], low[k, rows, :]
        facing = dot(jnp.concatenate((ohi, olo), axis=0), hi, ((1,), (1,)))
        facing = facing[:SR] + facing[SR:] + dot(ohi, lo, ((1,), (1,)))
        ls[k] = stat_decay * ls[k] + w * facing
        chi, clo = high[k, :, lanes], low[k, :, lanes]
        term[...] = (dot(chi, hi, ((0,), (0,))) + dot(clo, hi, ((0,), (0,)))
                     + dot(chi, lo, ((0,), (0,))))
        rs[k] = stat_decay * rs[k] + w * term[side, :]
        pltpu.make_async_copy(ls.at[k], left_new.at[k], osem.at[0, k]).start()
        pltpu.make_async_copy(rs.at[k], right_new.at[k], osem.at[1, k]).start()
        return 0

    lax.fori_loop(0, NS, make_stats, 0)
    exchange_wait(me, send, recv, ssem, rsem)

    def take(j, _):
        code = recv[owner_of[j]]
        scales = scale_of(code[256:272, :])
        for n in range(4):
            update[j, :, n * CH:n * CH + CH] = (
                widen(code[n * SR:n * SR + SR, :]) * scales[n:n + 1, :])
        return 0

    lax.fori_loop(0, NB, take, 0)

    def done(k, _):
        pltpu.make_async_copy(ls.at[k], left_new.at[k], osem.at[0, k]).wait()
        pltpu.make_async_copy(rs.at[k], right_new.at[k], osem.at[1, k]).wait()
        return 0

    lax.fori_loop(0, NS, done, 0)
    gather.end()


def back(slot_of, owner_of, weight, slots, rfull, left_root, left_stat, right_stat):
    smem = pl.BlockSpec(memory_space=pltpu.SMEM)
    hbm = pl.BlockSpec(memory_space=pl.ANY)
    return pl.pallas_call(
        back_kernel,
        out_shape=(
            jax.ShapeDtypeStruct((NS, SR, BO), f32),
            jax.ShapeDtypeStruct((NS, SR, BO), f32),
            jax.ShapeDtypeStruct((NB, SR, BO), f32),
        ),
        in_specs=[smem, smem, smem, hbm, hbm, hbm, hbm, hbm],
        out_specs=(hbm, hbm, pl.BlockSpec(memory_space=pltpu.VMEM)),
        scratch_shapes=[
            pltpu.VMEM((ND, NS, SLOT, CH), i16),
            pltpu.VMEM((NS, BO, BO), bf16),
            pltpu.VMEM((NS, BO, BO), bf16),
            pltpu.VMEM((ND, NS, SR, BO), bf16),
            pltpu.VMEM((NS, SR, BO), bf16),
            pltpu.VMEM((NS, SR, BO), f32),
            pltpu.VMEM((NS, SR, BO), f32),
            pltpu.VMEM((CH, BO), f32),
            pltpu.VMEM((NS, SLOT, CH), i16),
            pltpu.VMEM((NO, SLOT, CH), i16),
            pltpu.VMEM((NO, SLOT, CH), i16),
            pltpu.SemaphoreType.DMA((NO,)),
            pltpu.SemaphoreType.DMA((NO,)),
            pltpu.SemaphoreType.DMA((GATHER_SEMS,)),
            pltpu.SemaphoreType.DMA((GATHER_SEMS,)),
            pltpu.SemaphoreType.DMA((5,)),
            pltpu.SemaphoreType.DMA((2, NS)),
        ],
        compiler_params=pltpu.CompilerParams(
            collective_id=2, has_side_effects=True, vmem_limit_bytes=LIMIT),
        name="back",
    )(slot_of, owner_of, weight, slots, rfull, left_root, left_stat, right_stat)


def tables(plan):
    me = lax.axis_index("owner")
    table = plan.reshape(NO, NB)
    owner_of = lax.dynamic_index_in_dim(table, me, 0, keepdims=False)
    owners = jnp.arange(NO, dtype=i32)
    hit = (owners[:, None] == owner_of[None, :]).astype(i32)
    block_of = jnp.sum(hit * jnp.arange(NB, dtype=i32)[None, :], axis=1)
    holding = jnp.sum((table == me).astype(i32), axis=1)
    standing = jnp.cumsum(holding) - 1
    slot_of = jnp.clip(standing, 0, NS - 1)
    slot_ids = jnp.arange(NS, dtype=i32)
    match = ((slot_ids[:, None] == standing[None, :]) & (holding[None, :] > 0)).astype(i32)
    source_of = jnp.sum(match * owners[None, :], axis=1)
    weight = fresh_share * jnp.sum(match, axis=1).astype(f32)
    return owner_of, block_of, slot_of, source_of, weight


def local(grads, plan, left_stat, right_stat, left_root, right_root):
    owner_of, block_of, slot_of, source_of, weight = tables(plan)
    g7 = sum_over_dp(grads[0])
    slots, rfull = to_owners(block_of, source_of, g7, right_root[0])
    left_new, right_new, update = back(
        slot_of, owner_of, weight, slots, rfull, left_root[0], left_stat[0], right_stat[0])
    return left_new[None], right_new[None], update


def solution(mesh):
    return jax.shard_map(
        local,
        mesh=mesh,
        in_specs=(
            P("dp", "owner", None, None),
            P(),
            P("owner", None, "dp", None),
            P("owner", None, "dp", None),
            P("owner", None, "dp", None),
            P("owner", None, "dp", None),
        ),
        out_specs=(
            P("owner", None, "dp", None),
            P("owner", None, "dp", None),
            P("owner", "dp", None),
        ),
        check_vma=False,
    )
```

time: 418 us -> 203 us (0.49)
  the two profiles are of different devices: /device:TPU:122 before, /device:TPU:25 now
where the time goes in v1:
time: 203 us
  Pallas kernels  193 us (95%)
  local copies, waits for them, and re-layouts  6.5 us (3%)
  other arithmetic  2.63 us (1%)
    pallas_call x1, Pallas kernels, back(): pl.pallas_call(back_kernel, out_shape=(jax.ShapeDtypeStruct((NS, SR, BO),...  107 us
    pallas_call x1, Pallas kernels, to_owners(): pl.pallas_call(out_kernel, out_shape=(jax.ShapeDtypeStruct((NS, SLOT, CH)...  62.6 us
    pallas_call x1, Pallas kernels, sum_over_dp(): pl.pallas_call(sum_kernel, out_shape=jax.ShapeDtypeStruct((NB, SLOT, CH),...  23.6 us
    unnamed x9, local copies, waits for them, and re-layouts  5.63 us

profile of v1, /device:TPU:25, one launch (start us, length us, event | category | flops | bytes accessed | tf_op | source)
XLA Modules:
  0.0 202.9 jit_solution(2713446334125144289)
XLA Ops:
  0.6 0.8 reshape.34
  1.4 0.0 copy-start.2
  1.4 0.1 convert_reduce_fusion
  1.6 0.6 select_reduce_fusion.1.block_of
  2.2 0.1 copy.11
  2.3 0.1 reduce-window.7
  2.3 0.1 add_reduce_fusion
  2.4 0.5 broadcast_clamp_fusion.slot_of
  3.0 0.6 select_reduce_fusion
  3.6 0.6 convert_multiply_fusion.weight
  4.2 23.6 %sum_over_dp.1.g7 = s16[7,272,128]{2,1,0:T(8,128)(2,1)} custom-call(bf16[7,512,512]{2,1,0:T(8,128)(2,1)} %bitcast.10), custom_call_target="tpu_custom_call" | custom-call | tf_op jit(solution)/shard_map/sum_over_dp/pallas_call | solution.py:171
  27.7 0.0 copy-done.2
  27.8 62.6 %to_owners.1 = (s16[13,272,128]{2,1,0:T(8,128)(2,1)}, bf16[8,13,64,512]{3,2,1,0:T(8,128)(2,1)}) custom-call(s32[32]{0:T(128)} %select_reduce_fusion.1.block_of, s32[13]{0:T(128)} %get-tuple-element.13.source_of, s16[7,272,128]{2,1,0:T(8,128)(2,1)} %sum_over_dp.1.g7, bf16[13,64,512]{2,1,0:T(8,128)(2,1)} %bitcast.16), custom_call_target="tpu_custom_call" | custom-call | tf_op jit(solution)/shard_map/to_owners/pallas_call | solution.py:291
  90.4 106.9 %back.1 = (f32[13,64,512]{2,1,0:T(8,128)}, f32[13,64,512]{2,1,0:T(8,128)}, f32[7,64,512]{2,1,0:T(8,128)}) custom-call(s32[32]{0:T(128)} %broadcast_clamp_fusion.slot_of, s32[7]{0:T(128)} %copy-done.2, f32[13]{0:T(128)} %convert_multiply_fusion.weight, s16[13,272,128]{2,1,0:T(8,128)(2,1)} %get-tuple-element.8.slots, ...), custom_call_target="tpu_custom_call" | custom-call | tf_op jit(solution)/shard_map/back/pallas_call | solution.py:426
  197.3 0.0 copy-start
  197.3 2.9 %copy.15 = f32[1,13,64,512]{3,2,1,0:T(8,128)} copy(f32[1,13,64,512]{3,2,1,0:T(8,128)} %bitcast.14) | data formatting | bytes 3407872
  200.2 0.0 copy-done
  200.2 0.0 copy-start.1
  200.2 1.2 copy.16
  201.4 0.6 copy-done.1
  202.0 0.9 copy.17
  (2 shorter events, 0.0 us)
Async XLA Ops:
  1.4 26.3 %copy-start.2 = (s32[7]{0:T(128)}, s32[7]{0:T(128)S(1)}, u32[]{:S(2)}) copy-start(s32[7]{0:T(128)S(1)} %dynamic-slice_bitcast_fusion.owner_of) | copy-start | bytes 88
  197.3 2.9 %copy-start = (f32[13,64,512]{2,1,0:T(8,128)S(1)}, f32[13,64,512]{2,1,0:T(8,128)}, u32[]{:S(2)}) copy-start(f32[13,64,512]{2,1,0:T(8,128)} %get-tuple-element.11) | copy-start | bytes 5111812
  200.2 1.8 copy-start.1

commit v2 on v1

--- a/solution.py
+++ b/solution.py
@@ -63,15 +63,6 @@
 def greet(barrier, places):
     for place in places:
         pl.semaphore_signal(barrier, inc=1, device_id={"dp": place}, device_id_type=MESH)
-
-
-def greet_owners(barrier, me):
-    def one(k, _):
-        pl.semaphore_signal(
-            barrier, inc=1, device_id={"owner": (me + k) % NO}, device_id_type=MESH)
-        return 0
-
-    lax.fori_loop(1, NO, one, 0)
 
 
 def sum_kernel(grads, g7, own, par, snd, rcv, psend, precv, lsem, usend, urecv):
@@ -211,26 +202,35 @@
         self.la = self._go(3, src.at[a], full.at[dp, a], left)
         self.own = self._go(4, src, full.at[dp], partner)
 
-    def finish(self):
+    def stage(self, r):
         dp, x, c, partner, right, left, across = ring_places()
         a, b = slice(0, CUT), slice(CUT, NS)
         full = self.full
-        self.ra.wait_recv()
-        fa = self._go(5, full.at[left, a], full.at[left, a], right)
-        pa = self._go(6, full.at[left, a], full.at[left, a], partner)
-        self.lb.wait_recv()
-        fb = self._go(7, full.at[right, b], full.at[right, b], left)
-        pb = self._go(8, full.at[right, b], full.at[right, b], partner)
-        self.rb.wait_recv()
-        pc = self._go(9, full.at[left, b], full.at[left, b], partner)
-        self.la.wait_recv()
-        pd = self._go(10, full.at[right, a], full.at[right, a], partner)
-        fa.wait_recv()
-        pe = self._go(11, full.at[across, a], full.at[across, a], partner)
-        fb.wait_recv()
-        pf = self._go(12, full.at[across, b], full.at[across, b], partner)
-        for cp in (self.own, pa, pb, pc, pd, pe, pf):
-            cp.wait_recv()
+        if r == 0:
+            self.ra.wait_recv()
+            self.fa = self._go(5, full.at[left, a], full.at[left, a], right)
+            pa = self._go(6, full.at[left, a], full.at[left, a], partner)
+            self.lb.wait_recv()
+            self.fb = self._go(7, full.at[right, b], full.at[right, b], left)
+            pb = self._go(8, full.at[right, b], full.at[right, b], partner)
+            self.given = [self.own, pa, pb]
+        elif r == 1:
+            self.rb.wait_recv()
+            self.given.append(self._go(9, full.at[left, b], full.at[left, b], partner))
+            self.la.wait_recv()
+            self.given.append(self._go(10, full.at[right, a], full.at[right, a], partner))
+        elif r == 2:
+            self.fa.wait_recv()
+            self.given.append(self._go(11, full.at[across, a], full.at[across, a], partner))
+            self.fb.wait_recv()
+            self.given.append(self._go(12, full.at[across, b], full.at[across, b], partner))
+        else:
+            for cp in self.given:
+                cp.wait_recv()
+
+    def finish(self):
+        for r in range(4):
+            self.stage(r)
 
     def end(self):
         for cp in self.sent:
@@ -240,54 +240,123 @@
 GATHER_SEMS = 13
 
 
-def exchange_start(me, fetch, send, recv, ssem, rsem):
-    def one(k, _):
-        dest = (me + k) % NO
-        send[k] = fetch(dest)
-        remote(send.at[k], recv.at[me], ssem.at[k], rsem.at[k], {"owner": dest}).start()
-        return 0
-
-    lax.fori_loop(1, NO, one, 0)
-    recv[me] = fetch(me)
-
-
-def exchange_wait(me, send, recv, ssem, rsem):
-    def one(k, _):
-        came = (me + NO - k) % NO
-        cp = remote(send.at[k], recv.at[came], ssem.at[k], rsem.at[k], {"owner": came})
-        cp.wait_recv()
-        cp.wait_send()
-        return 0
-
-    lax.fori_loop(1, NO, one, 0)
-
-
-def out_kernel(block_of, source_of, g7, right_root, slots, rfull,
-               send, recv, ssem, rsem, gsend, grecv, lsem):
+NY = 4
+NZ = 8
+FRONT = slice(0, 4)
+REAR = slice(4, NB)
+
+
+def plane():
     me = lax.axis_index("owner")
+    z, y = me // NY, me % NY
+    return me, z, y, ((z + 1) % NZ) * NY + y, ((z + NZ - 1) % NZ) * NY + y
+
+
+def greet_plane(barrier):
+    me, z, y, up, down = plane()
+    places = [up, down] + [z * NY + (y + t) % NY for t in range(1, NY)]
+    for place in places:
+        pl.semaphore_signal(barrier, inc=1, device_id={"owner": place}, device_id_type=MESH)
+
+
+PEERS = 3 + 2 + NY - 1
+
+
+class Line:
+    def __init__(self, send, recv, towards):
+        self.send, self.recv, self.towards = send, recv, towards
+        self.copies = {}
+
+    def go(self, n, src, dst):
+        cp = remote(src, dst, self.send.at[n], self.recv.at[n], {"owner": self.towards})
+        cp.start()
+        self.copies[n] = cp
+
+    def came(self, *names):
+        for n in names:
+            self.copies[n].wait_recv()
+
+    def end(self):
+        for cp in self.copies.values():
+            cp.wait_send()
+
+
+def out_kernel(pick, source_of, g7, right_root, slots, rfull,
+               u1, u2, u3, d1, d2, d3, far, ysend, recv,
+               usem, ursem, dsem, drsem, ysem, yrsem, gsend, grecv, lsem):
+    me, z, y, up, down = plane()
     dp, x, c, partner, right, left, across = ring_places()
     barrier = pltpu.get_barrier_semaphore()
     greet(barrier, (partner, right, left))
-    greet_owners(barrier, me)
-    pl.semaphore_wait(barrier, 3 + NO - 1)
+    greet_plane(barrier)
+    pl.semaphore_wait(barrier, PEERS)
+    ups, downs = Line(usem, ursem, up), Line(dsem, drsem, down)
+    ups.go(0, g7.at[FRONT], u1.at[FRONT])
+    downs.go(0, g7.at[REAR], d1.at[REAR])
+    ups.go(1, g7.at[REAR], u1.at[REAR])
+    downs.go(1, g7.at[FRONT], d1.at[FRONT])
     gather = Gather(right_root, rfull, gsend, grecv)
     gather.begin()
     local = pltpu.make_async_copy(right_root, rfull.at[dp], lsem)
     local.start()
-    exchange_start(me, lambda dest: g7[block_of[dest]], send, recv, ssem, rsem)
-    gather.finish()
-    exchange_wait(me, send, recv, ssem, rsem)
-
-    def pick(k, _):
+    hand = []
+
+    def pass_on(n, ref, rel):
+        s = (z + rel) % NZ
+        for t in range(1, NY):
+            yy = (y + t) % NY
+            ysend[n, t - 1] = ref[pick[s * NY + yy]]
+            cp = remote(ysend.at[n, t - 1], recv.at[s * NY + y], ysem.at[n, t - 1],
+                        yrsem.at[n, t - 1], {"owner": z * NY + yy})
+            cp.start()
+            hand.append(cp)
+        recv[s * NY + y] = ref[pick[s * NY + y]]
+
+    pass_on(0, g7, 0)
+    steps = ((u1, u2, d1, d2, 7, 1), (u2, u3, d2, d3, 6, 2))
+    for r, (ua, ub, da, db, below, above) in enumerate(steps):
+        ups.came(2 * r)
+        ups.go(2 * r + 2, ua.at[FRONT], ub.at[FRONT])
+        downs.came(2 * r)
+        downs.go(2 * r + 2, da.at[REAR], db.at[REAR])
+        ups.came(2 * r + 1)
+        ups.go(2 * r + 3, ua.at[REAR], ub.at[REAR])
+        downs.came(2 * r + 1)
+        downs.go(2 * r + 3, da.at[FRONT], db.at[FRONT])
+        pass_on(2 * r + 1, ua, below)
+        pass_on(2 * r + 2, da, above)
+        gather.stage(r)
+    ups.came(4)
+    ups.go(6, u3.at[FRONT], far.at[FRONT])
+    downs.came(4)
+    downs.go(6, d3.at[REAR], far.at[REAR])
+    ups.came(5)
+    downs.came(5)
+    pass_on(5, u3, 5)
+    pass_on(6, d3, 3)
+    gather.stage(2)
+    ups.came(6)
+    downs.came(6)
+    pass_on(7, far, 4)
+    gather.stage(3)
+    for cp in hand:
+        cp.wait_recv()
+
+    def take(k, _):
         slots[k] = recv[source_of[k]]
         return 0
 
-    lax.fori_loop(0, NS, pick, 0)
+    lax.fori_loop(0, NS, take, 0)
+    for cp in hand:
+        cp.wait_send()
+    ups.end()
+    downs.end()
     gather.end()
     local.wait()
 
 
-def to_owners(block_of, source_of, g7, right_root):
+def to_owners(pick, source_of, g7, right_root):
+    coded = pltpu.VMEM((NB, SLOT, CH), i16)
     return pl.pallas_call(
         out_kernel,
         out_shape=(
@@ -305,10 +374,15 @@
             pl.BlockSpec(memory_space=pl.ANY),
         ),
         scratch_shapes=[
+            coded, coded, coded, coded, coded, coded, coded,
+            pltpu.VMEM((NZ, NY - 1, SLOT, CH), i16),
             pltpu.VMEM((NO, SLOT, CH), i16),
-            pltpu.VMEM((NO, SLOT, CH), i16),
-            pltpu.SemaphoreType.DMA((NO,)),
-            pltpu.SemaphoreType.DMA((NO,)),
+            pltpu.SemaphoreType.DMA((7,)),
+            pltpu.SemaphoreType.DMA((7,)),
+            pltpu.SemaphoreType.DMA((7,)),
+            pltpu.SemaphoreType.DMA((7,)),
+            pltpu.SemaphoreType.DMA((NZ, NY - 1)),
+            pltpu.SemaphoreType.DMA((NZ, NY - 1)),
             pltpu.SemaphoreType.DMA((GATHER_SEMS,)),
             pltpu.SemaphoreType.DMA((GATHER_SEMS,)),
             pltpu.SemaphoreType.DMA,
@@ -316,7 +390,7 @@
         compiler_params=pltpu.CompilerParams(
             collective_id=1, has_side_effects=True, vmem_limit_bytes=LIMIT),
         name="to_owners",
-    )(block_of, source_of, g7, right_root)
+    )(pick, source_of, g7, right_root)
 
 
 def dot(a, b, dims=((1,), (0,))):
@@ -328,11 +402,13 @@
     return hi, (v - hi.astype(f32)).astype(bf16)
 
 
-def back_kernel(slot_of, owner_of, weight, slots, rfull, left_root, left_stat, right_stat,
-                left_new, right_new, update,
-                codes, high, low, rv, lv, ls, rs, term, usl, send, recv,
-                ssem, rsem, gsend, grecv, lsem, osem):
-    me = lax.axis_index("owner")
+def back_kernel(slot_of, mine, column, above, weight, slots, rfull, left_root, left_stat,
+                right_stat, left_new, right_new, update,
+                codes, high, low, rv, lv, ls, rs, term, usl,
+                y0, y1, y2, y3, y4, y5, y6, y7, ysend,
+                ur0, ur1, ur2, ur3, dr0, dr1, dr2, dr3, ush, dsh,
+                usem, ursem, dsem, drsem, ysem, yrsem, gsend, grecv, lsem, osem):
+    me, z, y, up, down = plane()
     dp, x, c, partner, right, left, across = ring_places()
     loads = [
         pltpu.make_async_copy(slots, codes.at[dp], lsem.at[0]),
@@ -345,8 +421,8 @@
         cp.start()
     barrier = pltpu.get_barrier_semaphore()
     greet(barrier, (partner, right, left))
-    greet_owners(barrier, me)
-    pl.semaphore_wait(barrier, 3 + NO - 1)
+    greet_plane(barrier)
+    pl.semaphore_wait(barrier, PEERS)
     gather = Gather(slots, codes, gsend, grecv)
     gather.begin()
     gather.finish()
@@ -377,7 +453,6 @@
         return 0
 
     lax.fori_loop(0, NS, make_update, 0)
-    exchange_start(me, lambda dest: usl[slot_of[dest]], send, recv, ssem, rsem)
 
     rows = pl.ds(pl.multiple_of(dp * SR, SR), SR)
     lanes = pl.ds(pl.multiple_of(x * CH, CH), CH)
@@ -398,11 +473,107 @@
         pltpu.make_async_copy(rs.at[k], right_new.at[k], osem.at[1, k]).start()
         return 0
 
-    lax.fori_loop(0, NS, make_stats, 0)
-    exchange_wait(me, send, recv, ssem, rsem)
+    def stats(first, last):
+        lax.fori_loop(first, last, make_stats, 0)
+
+    ys = (y0, y1, y2, y3, y4, y5, y6, y7)
+    hand = {}
+
+    def across_y(n):
+        d = (z + n) % NZ
+        hand[n] = []
+        for t in range(1, NY):
+            yy = (y + t) % NY
+            ysend[n, t - 1] = usl[slot_of[d * NY + yy]]
+            cp = remote(ysend.at[n, t - 1], ys[n].at[y], ysem.at[n, t - 1],
+                        yrsem.at[n, t - 1], {"owner": z * NY + yy})
+            cp.start()
+            hand[n].append(cp)
+        ys[n][y] = usl[slot_of[d * NY + y]]
+
+    def across_done(n):
+        for cp in hand[n]:
+            cp.wait_recv()
+
+    ups, downs = Line(usem, ursem, up), Line(dsem, drsem, down)
+
+    def train(n, out, blocks, came):
+        d = (z + n) % NZ
+
+        def one(j, _):
+            here = ys[n][column[d * NB + j]]
+            if came is not None:
+                here = jnp.where(jnp.full((SLOT, CH), mine[d * NB + j], i32) > 0, here, came[j])
+            out[j] = here
+            return 0
+
+        lax.fori_loop(blocks.start, blocks.stop, one, 0)
+
+    across_y(4)
+    across_y(3)
+    across_y(5)
+    across_done(4)
+    train(4, ush.at[3], FRONT, None)
+    ups.go(0, ush.at[3, FRONT], ur3.at[FRONT])
+    train(4, dsh.at[3], REAR, None)
+    downs.go(0, dsh.at[3, REAR], dr3.at[REAR])
+    across_done(3)
+    train(3, ush.at[2], REAR, None)
+    ups.go(1, ush.at[2, REAR], ur2.at[REAR])
+    across_done(5)
+    train(5, dsh.at[2], FRONT, None)
+    downs.go(1, dsh.at[2, FRONT], dr2.at[FRONT])
+    across_y(2)
+    across_y(6)
+    stats(0, 3)
+    ups.came(0)
+    train(3, ush.at[2], FRONT, ur3)
+    ups.go(2, ush.at[2, FRONT], ur2.at[FRONT])
+    downs.came(0)
+    train(5, dsh.at[2], REAR, dr3)
+    downs.go(2, dsh.at[2, REAR], dr2.at[REAR])
+    across_y(1)
+    across_y(7)
+    across_done(2)
+    across_done(6)
+    ups.came(1)
+    train(2, ush.at[1], REAR, ur2)
+    ups.go(3, ush.at[1, REAR], ur1.at[REAR])
+    downs.came(1)
+    train(6, dsh.at[1], FRONT, dr2)
+    downs.go(3, dsh.at[1, FRONT], dr1.at[FRONT])
+    stats(3, 6)
+    ups.came(2)
+    train(2, ush.at[1], FRONT, ur2)
+    ups.go(4, ush.at[1, FRONT], ur1.at[FRONT])
+    downs.came(2)
+    train(6, dsh.at[1], REAR, dr2)
+    downs.go(4, dsh.at[1, REAR], dr1.at[REAR])
+    across_y(0)
+    across_done(1)
+    across_done(7)
+    ups.came(3)
+    train(1, ush.at[0], REAR, ur1)
+    ups.go(5, ush.at[0, REAR], ur0.at[REAR])
+    downs.came(3)
+    train(7, dsh.at[0], FRONT, dr1)
+    downs.go(5, dsh.at[0, FRONT], dr0.at[FRONT])
+    stats(6, 9)
+    ups.came(4)
+    train(1, ush.at[0], FRONT, ur1)
+    ups.go(6, ush.at[0, FRONT], ur0.at[FRONT])
+    downs.came(4)
+    train(7, dsh.at[0], REAR, dr1)
+    downs.go(6, dsh.at[0, REAR], dr0.at[REAR])
+    stats(9, NS)
+    across_done(0)
+    ups.came(5, 6)
+    downs.came(5, 6)
 
     def take(j, _):
-        code = recv[owner_of[j]]
+        shape = jnp.zeros((SLOT, CH), i32)
+        code = jnp.where(shape + above[j] > 0, dr0[j], ur0[j])
+        code = jnp.where(shape + mine[z * NB + j] > 0, y0[column[z * NB + j]], code)
         scales = scale_of(code[256:272, :])
         for n in range(4):
             update[j, :, n * CH:n * CH + CH] = (
@@ -417,10 +588,17 @@
         return 0
 
     lax.fori_loop(0, NS, done, 0)
+    for n in range(NZ):
+        for cp in hand[n]:
+            cp.wait_send()
+    ups.end()
+    downs.end()
     gather.end()
 
 
-def back(slot_of, owner_of, weight, slots, rfull, left_root, left_stat, right_stat):
+def back(slot_of, mine, column, above, weight, slots, rfull, left_root, left_stat, right_stat):
+    coded = pltpu.VMEM((NB, SLOT, CH), i16)
+    column_of = pltpu.VMEM((NY, SLOT, CH), i16)
     smem = pl.BlockSpec(memory_space=pltpu.SMEM)
     hbm = pl.BlockSpec(memory_space=pl.ANY)
     return pl.pallas_call(
@@ -430,7 +608,7 @@
             jax.ShapeDtypeStruct((NS, SR, BO), f32),
             jax.ShapeDtypeStruct((NB, SR, BO), f32),
         ),
-        in_specs=[smem, smem, smem, hbm, hbm, hbm, hbm, hbm],
+        in_specs=[smem, smem, smem, smem, smem, hbm, hbm, hbm, hbm, hbm],
         out_specs=(hbm, hbm, pl.BlockSpec(memory_space=pltpu.VMEM)),
         scratch_shapes=[
             pltpu.VMEM((ND, NS, SLOT, CH), i16),
@@ -442,10 +620,18 @@
             pltpu.VMEM((NS, SR, BO), f32),
             pltpu.VMEM((CH, BO), f32),
             pltpu.VMEM((NS, SLOT, CH), i16),
-            pltpu.VMEM((NO, SLOT, CH), i16),
-            pltpu.VMEM((NO, SLOT, CH), i16),
-            pltpu.SemaphoreType.DMA((NO,)),
-            pltpu.SemaphoreType.DMA((NO,)),
+            column_of, column_of, column_of, column_of,
+            column_of, column_of, column_of, column_of,
+            pltpu.VMEM((NZ, NY - 1, SLOT, CH), i16),
+            coded, coded, coded, coded, coded, coded, coded, coded,
+            pltpu.VMEM((4, NB, SLOT, CH), i16),
+            pltpu.VMEM((4, NB, SLOT, CH), i16),
+            pltpu.SemaphoreType.DMA((7,)),
+            pltpu.SemaphoreType.DMA((7,)),
+            pltpu.SemaphoreType.DMA((7,)),
+            pltpu.SemaphoreType.DMA((7,)),
+            pltpu.SemaphoreType.DMA((NZ, NY - 1)),
+            pltpu.SemaphoreType.DMA((NZ, NY - 1)),
             pltpu.SemaphoreType.DMA((GATHER_SEMS,)),
             pltpu.SemaphoreType.DMA((GATHER_SEMS,)),
             pltpu.SemaphoreType.DMA((5,)),
@@ -454,16 +640,23 @@
         compiler_params=pltpu.CompilerParams(
             collective_id=2, has_side_effects=True, vmem_limit_bytes=LIMIT),
         name="back",
-    )(slot_of, owner_of, weight, slots, rfull, left_root, left_stat, right_stat)
+    )(slot_of, mine, column, above, weight, slots, rfull, left_root, left_stat, right_stat)
 
 
 def tables(plan):
     me = lax.axis_index("owner")
+    z, y = me // NY, me % NY
     table = plan.reshape(NO, NB)
-    owner_of = lax.dynamic_index_in_dim(table, me, 0, keepdims=False)
     owners = jnp.arange(NO, dtype=i32)
-    hit = (owners[:, None] == owner_of[None, :]).astype(i32)
-    block_of = jnp.sum(hit * jnp.arange(NB, dtype=i32)[None, :], axis=1)
+    blocks = jnp.arange(NB, dtype=i32)
+    lane = lax.dynamic_index_in_dim(plan.reshape(NZ, NY, NB), y, 1, keepdims=False)
+    to_plane = z * NY + jnp.arange(NY, dtype=i32)
+    hit = (lane[:, None, :] == to_plane[None, :, None]).astype(i32)
+    pick = jnp.sum(hit * blocks[None, None, :], axis=2).reshape(-1)
+    mine = (lane // NY == z).astype(i32)
+    column = lane % NY
+    off = (lax.dynamic_index_in_dim(lane, z, 0, keepdims=False) // NY - z) % NZ
+    above = ((off < 4) | ((off == 4) & (blocks >= 4))).astype(i32)
     holding = jnp.sum((table == me).astype(i32), axis=1)
     standing = jnp.cumsum(holding) - 1
     slot_of = jnp.clip(standing, 0, NS - 1)
@@ -471,15 +664,16 @@
     match = ((slot_ids[:, None] == standing[None, :]) & (holding[None, :] > 0)).astype(i32)
     source_of = jnp.sum(match * owners[None, :], axis=1)
     weight = fresh_share * jnp.sum(match, axis=1).astype(f32)
-    return owner_of, block_of, slot_of, source_of, weight
+    return pick, mine.reshape(-1), column.reshape(-1), above, slot_of, source_of, weight
 
 
 def local(grads, plan, left_stat, right_stat, left_root, right_root):
-    owner_of, block_of, slot_of, source_of, weight = tables(plan)
+    pick, mine, column, above, slot_of, source_of, weight = tables(plan)
     g7 = sum_over_dp(grads[0])
-    slots, rfull = to_owners(block_of, source_of, g7, right_root[0])
+    slots, rfull = to_owners(pick, source_of, g7, right_root[0])
     left_new, right_new, update = back(
-        slot_of, owner_of, weight, slots, rfull, left_root[0], left_stat[0], right_stat[0])
+        slot_of, mine, column, above, weight,
+        slots, rfull, left_root[0], left_stat[0], right_stat[0])
     return left_new[None], right_new[None], update
 
 

time: 203 us -> 186 us (0.916)
  the two profiles are of different devices: /device:TPU:25 before, /device:TPU:8 now
where the time goes in v2:
time: 186 us; the launch traced here: 183 us
  Pallas kernels  169 us (91%)
  local copies, waits for them, and re-layouts  8.58 us (5%)
  other arithmetic  4.45 us (2%)
    pallas_call x1, Pallas kernels, back(): pl.pallas_call(back_kernel, out_shape=(jax.ShapeDtypeStruct((NS, SR, BO),...  91.9 us
    pallas_call x1, Pallas kernels, to_owners(): pl.pallas_call(out_kernel, out_shape=(jax.ShapeDtypeStruct((NS, SLOT, CH)...  54.3 us
    pallas_call x1, Pallas kernels, sum_over_dp(): pl.pallas_call(sum_kernel, out_shape=jax.ShapeDtypeStruct((NB, SLOT, CH),...  23.3 us
    unnamed x7, local copies, waits for them, and re-layouts  5.62 us

profile of v2, /device:TPU:8, one launch (start us, length us, event | category | flops | bytes accessed | tf_op | source)
XLA Modules:
  0.0 183.2 jit_solution(6955610444128579651)
XLA Ops:
  0.7 0.7 compare_convert_fusion.1
  1.4 0.1 reshape.55
  1.5 0.1 reduce_sum.36
  1.6 0.8 reshape.53
  2.4 0.6 or_convert_fusion.above
  3.0 0.5 broadcast.105
  3.5 0.7 fusion.2
  4.2 0.1 squeeze.23
  4.3 0.5 compare_convert_fusion.mine
  4.8 0.5 and_select_fusion.2.column
  5.3 0.1 copy.12
  5.4 0.1 select_reduce_fusion
  5.5 0.1 copy.13
  5.6 0.6 reshape.54.pick
  6.1 0.1 copy.11
  6.2 0.1 reduce-window.7
  6.3 0.1 add_reduce_fusion
  6.4 0.5 broadcast_clamp_fusion.slot_of
  6.9 0.6 select_reduce_fusion.1
  7.5 0.6 convert_multiply_fusion.weight
  8.1 23.3 %sum_over_dp.1.g7 = s16[7,272,128]{2,1,0:T(8,128)(2,1)} custom-call(bf16[7,512,512]{2,1,0:T(8,128)(2,1)} %bitcast.19), custom_call_target="tpu_custom_call" | custom-call | tf_op jit(solution)/shard_map/sum_over_dp/pallas_call | solution.py:162
  31.4 54.3 %to_owners.1 = (s16[13,272,128]{2,1,0:T(8,128)(2,1)}, bf16[8,13,64,512]{3,2,1,0:T(8,128)(2,1)}) custom-call(s32[32]{0:T(128)} %reshape.54.pick, s32[13]{0:T(128)} %get-tuple-element.13.source_of, s16[7,272,128]{2,1,0:T(8,128)(2,1)} %sum_over_dp.1.g7, bf16[13,64,512]{2,1,0:T(8,128)(2,1)} %bitcast.25), custom_call_target="tpu_custom_call" | custom-call | tf_op jit(solution)/shard_map/to_owners/pallas_call | solution.py:360
  85.7 91.9 %back.1 = (f32[13,64,512]{2,1,0:T(8,128)}, f32[13,64,512]{2,1,0:T(8,128)}, f32[7,64,512]{2,1,0:T(8,128)}) custom-call(s32[32]{0:T(128)} %broadcast_clamp_fusion.slot_of, s32[56]{0:T(128)} %compare_convert_fusion.mine, s32[56]{0:T(128)} %and_select_fusion.2.column, s32[7]{0:T(128)} %or_convert_fusion.above, f32[13]{0:T(128)} %convert_multiply_fusion.weight, ...), custom_call_target="tpu_custom_call" | custom-call | tf_op jit(solution)/shard_map/back/pallas_call | solution.py:604
  177.6 0.0 copy-start
  177.6 2.9 %copy.17 = f32[1,13,64,512]{3,2,1,0:T(8,128)} copy(f32[1,13,64,512]{3,2,1,0:T(8,128)} %bitcast.23) | data formatting | bytes 3407872
  180.5 0.0 copy-done
  180.5 0.0 copy-start.1
  180.5 1.2 copy.18
  181.7 0.6 copy-done.1
  182.3 0.9 copy.19
  (2 shorter events, 0.0 us)
Async XLA Ops:
  177.6 2.9 %copy-start = (f32[13,64,512]{2,1,0:T(8,128)S(1)}, f32[13,64,512]{2,1,0:T(8,128)}, u32[]{:S(2)}) copy-start(f32[13,64,512]{2,1,0:T(8,128)} %get-tuple-element.11) | copy-start | bytes 5111812
  180.5 1.8 copy-start.1

commit v3 on v0

v3 whole, which is shorter than its diff:
```python
import functools

import jax
import jax.numpy as jnp
from jax import lax
from jax.experimental import pallas as pl
from jax.experimental.pallas import tpu as pltpu
from jax.sharding import PartitionSpec as P

MESH = pl.DeviceIdType.MESH
f32 = jnp.float32
bf16 = jnp.bfloat16
i16 = jnp.int16
i32 = jnp.int32

stat_decay = 0.95
fresh_share = 0.05

NB = 7
NO = 32
NS = 13
ND = 8
SR = 64
BO = 512
CH = 128
NY = 4
NZ = 8
HALF = 144
SLOT = 272
UNIT = 912
FRONT = slice(0, 512)
REAR = slice(512, UNIT)
BACK = slice(512, 896)
SCALES = slice(896, UNIT)
LIMIT = 60 * 1024 * 1024


def encode(x):
    m = jnp.maximum(jnp.max(jnp.abs(x), axis=0, keepdims=True), 2.0 ** -100)
    e = jnp.floor(jnp.log2(m) * 256.0) + 1.0
    q = jnp.round(x * (32700.0 * jnp.exp2(e * (-1.0 / 256.0))))
    return q.astype(i32).astype(i16), e


def scale_of(e16):
    return jnp.exp2(e16.astype(i32).astype(f32) * (1.0 / 256.0)) * (1.0 / 32700.0)


def widen(q):
    return q.astype(i32).astype(f32)


def remote(src, dst, send, recv, where):
    return pltpu.make_async_remote_copy(
        src_ref=src, dst_ref=dst, send_sem=send, recv_sem=recv,
        device_id=where, device_id_type=MESH)


def dot(a, b, dims=((1,), (0,))):
    return lax.dot_general(a, b, (dims, ((), ())), preferred_element_type=f32)


def split(v):
    hi = v.astype(bf16)
    return hi, (v - hi.astype(f32)).astype(bf16)


def rows_of(t, n=SR):
    return pl.ds(pl.multiple_of(t * n, n), n)


def shampoo_kernel(plan, grads, left_stat, right_stat, left_root, right_root,
                   left_new, right_new, update, *scratch):
    it = iter(scratch)
    slot_of, source_of, block_at, weight = (next(it) for _ in range(4))
    own, par, snd, rcv = (next(it) for _ in range(4))
    unit = [next(it) for _ in range(2)]
    hops = [[next(it) for _ in range(7)] for _ in range(2)]
    ysend, got, xs, gx = ([next(it) for _ in range(2)] for _ in range(4))
    lf, rf, ghi, glo, phi, plo = (next(it) for _ in range(6))
    xu, ux = ([next(it) for _ in range(2)] for _ in range(2))
    ybuf = [[next(it) for _ in range(8)] for _ in range(2)]
    yback = [next(it) for _ in range(2)]
    ur = [[next(it) for _ in range(4)] for _ in range(2)]
    dr = [[next(it) for _ in range(4)] for _ in range(2)]
    ush = [next(it) for _ in range(2)]
    dsh = [next(it) for _ in range(2)]
    sx, sr = ([next(it) for _ in range(2)] for _ in range(2))
    ls, rs, shelf = next(it), next(it), next(it)
    pair_sem, load_sem, unit_sem, line_sem, y_sem, x_sem, out_sem = (next(it) for _ in range(7))

    me = lax.axis_index("owner")
    z, y = me // NY, me % NY
    up, down = ((z + 1) % NZ) * NY + y, ((z + NZ - 1) % NZ) * NY + y
    dp = lax.axis_index("dp")
    x, c = dp // 2, dp % 2
    partner = x * 2 + 1 - c
    right = ((x + 1) % 4) * 2 + c
    left = ((x + 3) % 4) * 2 + c
    row_id = lax.broadcasted_iota(i32, (16, CH), 0)
    sent = []

    mine = {}
    for n, off in ((0, 2), (2, 3), (1, 1), (3, 0)):
        t = ((x + off) % 4) * 2 + c
        mine[n] = pltpu.make_async_copy(grads.at[:, rows_of(t), :], own.at[n], load_sem.at[n])
        mine[n].start()
    stat_in = [pltpu.make_async_copy(left_stat, ls, load_sem.at[4]),
               pltpu.make_async_copy(right_stat, rs, load_sem.at[5])]
    root_in = []
    for i in range(2):
        k = (dp + 8 * i) % NS
        root_in.append(pltpu.make_async_copy(
            left_root.at[k], lf.at[i, rows_of(dp)], load_sem.at[6 + i]))
        root_in.append(pltpu.make_async_copy(
            right_root.at[k], rf.at[i, rows_of(dp)], load_sem.at[8 + i]))

    barrier = pltpu.get_barrier_semaphore()
    for t in range(1, ND):
        pl.semaphore_signal(
            barrier, inc=1, device_id={"dp": (dp + t) % ND}, device_id_type=MESH)
    for place in [up, down] + [z * NY + (y + t) % NY for t in range(1, NY)]:
        pl.semaphore_signal(barrier, inc=1, device_id={"owner": place}, device_id_type=MESH)
    pl.semaphore_wait(barrier, ND - 1 + 2 + NY - 1)

    pair = {}
    for n, off in ((0, 2), (2, 3), (1, 1), (3, 0)):
        t = ((x + off) % 4) * 2 + 1 - c
        pair[n] = remote(grads.at[:, rows_of(t), :], par.at[n],
                         pair_sem.at[0, n], pair_sem.at[1, n], {"dp": partner})
        pair[n].start()
        sent.append(pair[n])
    for cp in root_in + stat_in:
        cp.start()

    def stand(i, count):
        hold, which = jnp.int32(0), jnp.int32(0)
        for j in range(NB):
            hit = (plan[i * NB + j] == me).astype(i32)
            hold = hold + hit * (1 - hold)
            which = which + hit * (j - which)
        slot_of[i] = count * (count < NS).astype(i32)
        source_of[NS + i] = hold * (count + 1) - 1
        block_at[NS + i] = which
        return count + hold

    count = lax.fori_loop(0, NO, stand, jnp.int32(0))

    def place(k, _):
        def look(i, found):
            hit = (source_of[NS + i] == k).astype(i32)
            return found[0] + hit * (i - found[0]), found[1] + hit * (block_at[NS + i] - found[1])

        src, blk = lax.fori_loop(0, NO, look, (jnp.int32(0), jnp.int32(0)))
        source_of[k] = src
        block_at[k] = blk
        weight[k] = fresh_share * (k < count).astype(i32).astype(f32)
        return 0

    lax.fori_loop(0, NS, place, 0)

    def pair_sum(n, j, k):
        cols = slice(k * CH, k * CH + CH)
        return own[n, j, :, cols].astype(f32) + par[n, j, :, cols].astype(f32)

    def unit_rows(j, kk):
        return pl.ds(pl.multiple_of(j * 128 + kk * SR, SR), SR)

    def scale_row(scales, r):
        return jnp.sum(jnp.where(row_id == r, scales, 0.0), axis=0, keepdims=True)

    def received(u, j, kk):
        row = scale_row(scale_of(rcv[u, 896:912, :]), j * 2 + kk)
        return widen(rcv[u, unit_rows(j, kk), :]) * row

    def fill(out, value):
        def block(j, sc):
            for kk in range(2):
                q, e = encode(value(j, kk))
                out[unit_rows(j, kk), :] = q
                sc = jnp.where(row_id == j * 2 + kk, e, sc)
            return sc

        sc = lax.fori_loop(0, NB, block, jnp.zeros((16, CH), f32))
        out[896:912, :] = sc.astype(i32).astype(i16)

    def ship(u, to):
        cp = remote(snd.at[u], rcv.at[u], unit_sem.at[0, u], unit_sem.at[1, u], {"dp": to})
        cp.start()
        sent.append(cp)
        return cp

    def ready(n):
        mine[n].wait()
        pair[n].wait_recv()

    class Line:
        def __init__(self, h, way, towards):
            self.h, self.way, self.towards = h, way, towards
            self.copies = {}

        def go(self, n, src, dst):
            cp = remote(src, dst, line_sem.at[self.h, self.way, 0, n],
                        line_sem.at[self.h, self.way, 1, n], {"owner": self.towards})
            cp.start()
            sent.append(cp)
            self.copies[n] = cp

        def came(self, *names):
            for n in names:
                self.copies[n].wait_recv()

    class Outward:
        def __init__(self, h):
            self.h = h
            self.u1, self.u2, self.u3, self.d1, self.d2, self.d3, self.far = hops[h]
            self.ups, self.downs = Line(h, 0, up), Line(h, 1, down)
            self.hand, self.given = [], []

        def pass_on(self, n, ref, rel):
            h = self.h
            s = (z + rel) % NZ
            src = s * NY + y

            def code(yy):
                j = jnp.int32(0)
                for b in range(NB):
                    j = j + (plan[src * NB + b] == z * NY + yy).astype(i32) * (b - j)
                return shelf[j]

            for b in range(NB):
                shelf[b] = ref[b * 128:b * 128 + 128, :]
            scales = ref[896:912, :]
            for t in range(1, NY):
                yy = (y + t) % NY
                ysend[h][n, t - 1, 0:128, :] = code(yy)
                ysend[h][n, t - 1, 128:HALF, :] = scales
                cp = remote(ysend[h].at[n, t - 1], got[h].at[src], y_sem.at[h, 0, n, t - 1],
                            y_sem.at[h, 1, n, t - 1], {"owner": z * NY + yy})
                cp.start()
                sent.append(cp)
                self.hand.append(cp)
            got[h][src, 0:128, :] = code(y)
            got[h][src, 128:HALF, :] = scales

        def start(self):
            g = unit[self.h]
            self.ups.go(0, g.at[FRONT], self.u1.at[FRONT])
            self.downs.go(0, g.at[REAR], self.d1.at[REAR])
            self.ups.go(1, g.at[REAR], self.u1.at[REAR])
            self.downs.go(1, g.at[FRONT], self.d1.at[FRONT])
            self.pass_on(0, g, 0)

        def step(self, r):
            ups, downs = self.ups, self.downs
            if r < 3:
                ua, ub = ((self.u1, self.u2), (self.u2, self.u3))[r - 1]
                da, db = ((self.d1, self.d2), (self.d2, self.d3))[r - 1]
                ups.came(2 * r - 2)
                ups.go(2 * r, ua.at[FRONT], ub.at[FRONT])
                downs.came(2 * r - 2)
                downs.go(2 * r, da.at[REAR], db.at[REAR])
                ups.came(2 * r - 1)
                ups.go(2 * r + 1, ua.at[REAR], ub.at[REAR])
                downs.came(2 * r - 1)
                downs.go(2 * r + 1, da.at[FRONT], db.at[FRONT])
                self.pass_on(2 * r - 1, ua, NZ - r)
                self.pass_on(2 * r, da, r)
            else:
                ups.came(4)
                ups.go(6, self.u3.at[FRONT], self.far.at[FRONT])
                downs.came(4)
                downs.go(6, self.d3.at[REAR], self.far.at[REAR])
                ups.came(5)
                downs.came(5)
                self.pass_on(5, self.u3, 5)
                self.pass_on(6, self.d3, 3)

        def last(self):
            self.ups.came(6)
            self.downs.came(6)
            self.pass_on(7, self.far, 4)

        def spread(self):
            h = self.h
            for cp in self.hand:
                cp.wait_recv()
            for i in range(2):
                for t in (4, 3, 5, 2, 6, 1, 7, 0):
                    to = (dp + t) % ND
                    k = (to + 8 * i) % NS
                    if t == 0:
                        gx[h][i, dp] = got[h][source_of[k]]
                        continue
                    xs[h][i, t] = got[h][source_of[k]]
                    cp = remote(xs[h].at[i, t], gx[h].at[i, dp], x_sem.at[h, 0, i, t],
                                x_sem.at[h, 1, i, t], {"dp": to})
                    cp.start()
                    sent.append(cp)
                    self.given.append(cp)

        def open(self):
            h = self.h
            for cp in self.given:
                cp.wait_recv()
            for i in range(2):
                blk = block_at[(dp + 8 * i) % NS]

                def stripe(t, _):
                    scales = scale_of(gx[h][i, t, 128:HALF, :])
                    for kk in range(2):
                        v = (widen(gx[h][i, t, kk * SR:kk * SR + SR, :])
                             * scale_row(scales, blk * 2 + kk))
                        hi, lo = split(v)
                        cols = slice((2 * h + kk) * CH, (2 * h + kk + 1) * CH)
                        ghi[i, rows_of(t), cols] = hi
                        glo[i, rows_of(t), cols] = lo
                    return 0

                lax.fori_loop(0, ND, stripe, 0)

        def project(self):
            cols = slice(256 * self.h, 256 * self.h + 256)

            def part(m, _):
                i, rows = m // 2, rows_of(m % 2, 256)
                p = dot(lf[i, rows, :], ghi[i, :, cols]) + dot(lf[i, rows, :], glo[i, :, cols])
                hi, lo = split(p)
                phi[i, rows, cols] = hi
                plo[i, rows, cols] = lo
                return 0

            lax.fori_loop(0, 4, part, 0)

    class Train:
        def __init__(self, h, way, towards, land, out, ascending):
            self.h, self.land, self.out, self.ascending = h, land, out, ascending
            self.line = Line(h, way, towards)

        def place(self, r):
            return r if self.ascending else NZ - r

        def part(self, r, front, came):
            h, out = self.h, self.out
            src = ((z + self.place(r)) % NZ) * NY + y
            first, last, cut = (0, 4, FRONT) if front else (4, NB, BACK)

            def one(j, _):
                rows = pl.ds(pl.multiple_of(j * 128, 128), 128)
                o = plan[src * NB + j]
                new = ybuf[h][self.place(r)][lax.rem(o, NY)][0:128, :]
                if came is not None:
                    at = jnp.full((128, CH), (lax.div(o, NY) == z).astype(i32), i32)
                    new = jnp.where(at > 0, new.astype(i32), came[rows, :].astype(i32)).astype(i16)
                out[r - 1, rows, :] = new
                return 0

            lax.fori_loop(first, last, one, 0)
            return out.at[r - 1, cut], self.land[r - 1].at[cut]

        def scales(self, r, came):
            h, out = self.h, self.out
            src = ((z + self.place(r)) % NZ) * NY + y
            tile = jnp.zeros((16, CH), i32) if came is None else came[SCALES, :].astype(i32)
            for j in range(NB):
                o = plan[src * NB + j]
                new = ybuf[h][self.place(r)][lax.rem(o, NY)][128:HALF, :].astype(i32)
                at = (row_id // 2 == j).astype(i32) * (lax.div(o, NY) == z).astype(i32)
                tile = jnp.where(at > 0, new, tile)
            out[r - 1, SCALES, :] = tile.astype(i16)
            return out.at[r - 1, SCALES], self.land[r - 1].at[SCALES]

        def head(self, r):
            came = None
            if r < 3:
                self.line.came(2 * (2 - r) + 1)
                came = self.land[r]
            self.line.go(2 * (3 - r) + 1, *self.part(r, not self.ascending, came))

        def tail(self, r):
            came = None
            if r < 4:
                self.line.came(2 * (2 - r) + 2, 10 - r)
                came = self.land[r]
            self.line.go(2 * (3 - r) + 2, *self.part(r, self.ascending, came))
            self.line.go(11 - r, *self.scales(r, came))

        def arrived(self):
            self.line.came(5, 6, 10)

    class Inward:
        def __init__(self, h):
            self.h = h
            self.ups = Train(h, 2, up, ur[h], ush[h], True)
            self.downs = Train(h, 3, down, dr[h], dsh[h], False)
            self.hand, self.given = {}, []

        def multiply(self):
            h = self.h
            cols = slice(256 * h, 256 * h + 256)
            for i in range(2):
                def pairs(m, _):
                    b = (x + 2 + m) % 4
                    rows = rows_of(b, 128)
                    r = dot(jnp.concatenate((phi[i, rows, :], plo[i, rows, :]), axis=0),
                            rf[i, :, cols])
                    u = r[:128] + r[128:]
                    for cc in range(2):
                        sc = jnp.zeros((16, CH), f32)
                        for kk in range(2):
                            q, e = encode(u[cc * SR:cc * SR + SR, kk * CH:kk * CH + CH])
                            xu[h][i, b * 2 + cc, kk * SR:kk * SR + SR, :] = q
                            sc = jnp.where(row_id % 2 == kk, e, sc)
                        xu[h][i, b * 2 + cc, 128:HALF, :] = sc.astype(i32).astype(i16)
                    return 0

                lax.fori_loop(0, 4, pairs, 0)
                ux[h][dp + 8 * i] = xu[h][i, dp]
                for t in (4, 3, 5, 2, 6, 1, 7):
                    to = (dp + t) % ND
                    cp = remote(xu[h].at[i, to], ux[h].at[dp + 8 * i], x_sem.at[2 + h, 0, i, t],
                                x_sem.at[2 + h, 1, i, t], {"dp": to})
                    cp.start()
                    sent.append(cp)
                    self.given.append(cp)

        def arrive(self):
            for cp in self.given:
                cp.wait_recv()

        def across(self, n):
            h = self.h
            d = (z + n) % NZ
            self.hand[n] = []
            for t in range(1, NY):
                yy = (y + t) % NY
                yback[h][n, t - 1] = ux[h][slot_of[d * NY + yy]]
                cp = remote(yback[h].at[n, t - 1], ybuf[h][n].at[y], y_sem.at[2 + h, 0, n, t - 1],
                            y_sem.at[2 + h, 1, n, t - 1], {"owner": z * NY + yy})
                cp.start()
                sent.append(cp)
                self.hand[n].append(cp)
            ybuf[h][n][y] = ux[h][slot_of[d * NY + y]]

        def crossed(self, n):
            for cp in self.hand[n]:
                cp.wait_recv()

        def begin(self):
            self.across(4)
            self.across(3)
            self.across(5)

        def one(self):
            self.crossed(4)
            self.ups.tail(4)
            self.downs.tail(4)
            self.crossed(3)
            self.ups.head(3)
            self.crossed(5)
            self.downs.head(3)
            self.across(2)
            self.across(6)

        def two(self):
            self.ups.tail(3)
            self.downs.tail(3)
            self.across(1)
            self.across(7)
            self.crossed(2)
            self.ups.head(2)
            self.crossed(6)
            self.downs.head(2)

        def three(self):
            self.ups.tail(2)
            self.downs.tail(2)
            self.across(0)
            self.crossed(1)
            self.ups.head(1)
            self.crossed(7)
            self.downs.head(1)

        def four(self):
            self.ups.tail(1)
            self.downs.tail(1)

        def finish(self):
            h = self.h
            self.crossed(0)
            self.ups.arrived()
            self.downs.arrived()

            def take(j, _):
                o = plan[me * NB + j]
                near = ybuf[h][0][lax.rem(o, NY)]
                off = lax.rem(lax.div(o, NY) + NZ - z, NZ)
                above = (off < 4).astype(i32) + (off == 4).astype(i32) * (j >= 4).astype(i32)
                full = jnp.zeros((128, CH), i32)
                rows = pl.ds(pl.multiple_of(j * 128, 128), 128)
                local = (off == 0).astype(i32)
                code = jnp.where(full + above > 0, dr[h][0][rows, :].astype(i32),
                                 ur[h][0][rows, :].astype(i32))
                code = jnp.where(full + local > 0,
                                 near[0:128, :].astype(i32), code)
                tile = jnp.where(row_id * 0 + above > 0, dr[h][0][SCALES, :].astype(i32),
                                 ur[h][0][SCALES, :].astype(i32))
                tile = jnp.where(row_id * 0 + local > 0,
                                 near[128:HALF, :].astype(i32), tile)
                tile = scale_of(tile)
                for kk in range(2):
                    update[j, :, (2 * h + kk) * CH:(2 * h + kk + 1) * CH] = (
                        code[kk * SR:kk * SR + SR].astype(f32) * scale_row(tile, j * 2 + kk))
                return 0

            lax.fori_loop(0, NB, take, 0)

    stat_came = [[], []]

    def stat(which, i):
        def block(m, _):
            b = (x + 1 + m) % 4
            if which == 0:
                ohi, olo = ghi[i, rows_of(b, 128), :], glo[i, rows_of(b, 128), :]
                f = dot(jnp.concatenate((ohi, olo), axis=0), ghi[i], ((1,), (1,)))
                f = f[:128] + f[128:] + dot(ohi, glo[i], ((1,), (1,)))
            else:
                chi, clo = ghi[i, :, rows_of(b, 128)], glo[i, :, rows_of(b, 128)]
                f = (dot(chi, ghi[i], ((0,), (0,))) + dot(clo, ghi[i], ((0,), (0,)))
                     + dot(chi, glo[i], ((0,), (0,))))
            for cc in range(2):
                sc = jnp.zeros((16, CH), f32)
                for n in range(4):
                    q, e = encode(f[cc * SR:cc * SR + SR, n * CH:n * CH + CH])
                    sx[which][i, b * 2 + cc, n * SR:n * SR + SR, :] = q
                    sc = jnp.where(row_id == n, e, sc)
                sx[which][i, b * 2 + cc, 256:SLOT, :] = sc.astype(i32).astype(i16)
            return 0

        lax.fori_loop(0, 4, block, 0)
        sr[which][dp + 8 * i] = sx[which][i, dp]
        for t in (4, 3, 5, 2, 6, 1, 7):
            to = (dp + t) % ND
            cp = remote(sx[which].at[i, to], sr[which].at[dp + 8 * i], x_sem.at[4 + which, 0, i, t],
                        x_sem.at[4 + which, 1, i, t], {"dp": to})
            cp.start()
            sent.append(cp)
            stat_came[which].append(cp)

    def renew(which, held, out):
        for cp in stat_came[which]:
            cp.wait_recv()

        def slot(k, _):
            w = weight[k]
            scales = scale_of(sr[which][k, 256:SLOT, :])
            for n in range(4):
                cols = slice(n * CH, n * CH + CH)
                term = widen(sr[which][k, n * SR:n * SR + SR, :]) * scales[n:n + 1, :]
                held[k, :, cols] = stat_decay * held[k, :, cols] + w * term
            pltpu.make_async_copy(held.at[k], out.at[k], out_sem.at[which, k]).start()
            return 0

        lax.fori_loop(0, NS, slot, 0)

    out0, out1, in0, in1 = Outward(0), Outward(1), Inward(0), Inward(1)

    ready(0)
    fill(snd.at[0], lambda j, kk: pair_sum(0, j, kk))
    c0 = ship(0, right)
    ready(2)
    fill(snd.at[3], lambda j, kk: pair_sum(2, j, kk))
    c3 = ship(3, left)
    fill(snd.at[1], lambda j, kk: pair_sum(0, j, 2 + kk))
    c1 = ship(1, left)
    ready(1)
    c0.wait_recv()
    fill(snd.at[4], lambda j, kk: pair_sum(1, j, kk) + received(0, j, kk))
    c4 = ship(4, right)
    fill(snd.at[2], lambda j, kk: pair_sum(1, j, 2 + kk))
    c2 = ship(2, right)
    c1.wait_recv()
    fill(snd.at[5], lambda j, kk: pair_sum(2, j, 2 + kk) + received(1, j, kk))
    c5 = ship(5, left)
    ready(3)
    c3.wait_recv()
    c4.wait_recv()
    fill(unit[0], lambda j, kk: pair_sum(3, j, kk) + received(4, j, kk) + received(3, j, kk))
    out0.start()
    c2.wait_recv()
    c5.wait_recv()
    fill(unit[1], lambda j, kk: pair_sum(3, j, 2 + kk) + received(2, j, kk) + received(5, j, kk))
    roots = []
    for which, (src, dst) in enumerate(((left_root, lf), (right_root, rf))):
        for i in range(2):
            for t in range(1, ND):
                to = (dp + t) % ND
                cp = remote(src.at[(to + 8 * i) % NS], dst.at[i, rows_of(dp)],
                            x_sem.at[6 + which, 0, i, t], x_sem.at[6 + which, 1, i, t], {"dp": to})
                cp.start()
                sent.append(cp)
                roots.append(cp)
    out0.step(1)
    out0.step(2)
    out0.step(3)
    out1.start()
    out0.last()
    out1.step(1)
    out0.spread()
    out1.step(2)
    out0.open()
    out1.step(3)
    for cp in root_in:
        cp.wait()
    for cp in roots:
        cp.wait_recv()
    out0.project()
    out1.last()
    out1.spread()
    out1.open()
    out1.project()
    in0.multiply()
    in1.multiply()
    in0.arrive()
    in0.begin()
    in0.one()
    in1.arrive()
    stat(0, 0)
    in0.two()
    stat(1, 0)
    in0.three()
    stat(0, 1)
    in0.four()
    in1.begin()
    in1.one()
    stat(1, 1)
    in0.finish()
    in1.two()
    for cp in stat_in:
        cp.wait()
    renew(0, ls, left_new)
    in1.three()
    renew(1, rs, right_new)
    in1.four()
    in1.finish()

    def done(k, _):
        pltpu.make_async_copy(ls.at[k], left_new.at[k], out_sem.at[0, k]).wait()
        pltpu.make_async_copy(rs.at[k], right_new.at[k], out_sem.at[1, k]).wait()
        return 0

    lax.fori_loop(0, NS, done, 0)
    for cp in sent:
        cp.wait_send()


def shampoo(plan, grads, left_stat, right_stat, left_root, right_root):
    hbm = pl.BlockSpec(memory_space=pl.ANY)
    vmem = pltpu.VMEM
    unit = vmem((UNIT, CH), i16)
    return pl.pallas_call(
        shampoo_kernel,
        out_shape=(
            jax.ShapeDtypeStruct((NS, SR, BO), f32),
            jax.ShapeDtypeStruct((NS, SR, BO), f32),
            jax.ShapeDtypeStruct((NB, SR, BO), f32),
        ),
        in_specs=[pl.BlockSpec(memory_space=pltpu.SMEM), hbm, hbm, hbm, hbm, hbm],
        out_specs=(hbm, hbm, pl.BlockSpec(memory_space=vmem)),
        scratch_shapes=[
            pltpu.SMEM((NO,), i32),
            pltpu.SMEM((NS + NO,), i32),
            pltpu.SMEM((NS + NO,), i32),
            pltpu.SMEM((NS,), f32),
            vmem((4, NB, SR, BO), bf16),
            vmem((4, NB, SR, BO), bf16),
            vmem((6, UNIT, CH), i16),
            vmem((6, UNIT, CH), i16),
            *[unit] * 2,
            *[unit] * 14,
            *[vmem((NZ, NY - 1, HALF, CH), i16)] * 2,
            *[vmem((NO, HALF, CH), i16)] * 2,
            *[vmem((2, ND, HALF, CH), i16)] * 2,
            *[vmem((2, ND, HALF, CH), i16)] * 2,
            *[vmem((2, BO, BO), bf16)] * 6,
            *[vmem((2, ND, HALF, CH), i16)] * 2,
            *[vmem((2 * ND, HALF, CH), i16)] * 2,
            *[vmem((NY, HALF, CH), i16)] * 16,
            *[vmem((NZ, NY - 1, HALF, CH), i16)] * 2,
            *[unit] * 16,
            *[vmem((4, UNIT, CH), i16)] * 4,
            *[vmem((2, ND, SLOT, CH), i16)] * 2,
            *[vmem((2 * ND, SLOT, CH), i16)] * 2,
            vmem((NS, SR, BO), f32),
            vmem((NS, SR, BO), f32),
            vmem((NB, 128, CH), i16),
            pltpu.SemaphoreType.DMA((2, 4)),
            pltpu.SemaphoreType.DMA((10,)),
            pltpu.SemaphoreType.DMA((2, 6)),
            pltpu.SemaphoreType.DMA((2, 4, 2, 11)),
            pltpu.SemaphoreType.DMA((4, 2, NZ, NY - 1)),
            pltpu.SemaphoreType.DMA((8, 2, 2, ND)),
            pltpu.SemaphoreType.DMA((2, NS)),
        ],
        compiler_params=pltpu.CompilerParams(
            collective_id=0, has_side_effects=True, vmem_limit_bytes=LIMIT),
        name="shampoo",
    )(plan, grads, left_stat, right_stat, left_root, right_root)


def local(grads, plan, left_stat, right_stat, left_root, right_root):
    left_new, right_new, update = shampoo(
        plan, grads[0], left_stat[0], right_stat[0], left_root[0], right_root[0])
    return left_new[None], right_new[None], update


def solution(mesh):
    return jax.shard_map(
        local,
        mesh=mesh,
        in_specs=(
            P("dp", "owner", None, None),
            P(),
            P("owner", None, "dp", None),
            P("owner", None, "dp", None),
            P("owner", None, "dp", None),
            P("owner", None, "dp", None),
        ),
        out_specs=(
            P("owner", None, "dp", None),
            P("owner", None, "dp", None),
            P("owner", "dp", None),
        ),
        check_vma=False,
    )
```

time: 418 us -> 152 us (0.36)
  the two profiles are of different devices: /device:TPU:122 before, /device:TPU:8 now
where the time goes in v3:
time: 152 us; the launch traced here: 151 us
  Pallas kernels  145 us (95%)
  local copies, waits for them, and re-layouts  5.62 us (4%)
    pallas_call x1, Pallas kernels, shampoo(): pl.pallas_call(shampoo_kernel, out_shape=(jax.ShapeDtypeStruct((NS, SR, B...  145 us
    unnamed x7, local copies, waits for them, and re-layouts  5.62 us

profile of v3, /device:TPU:8, one launch (start us, length us, event | category | flops | bytes accessed | tf_op | source)
XLA Modules:
  0.0 151.4 jit_solution(4310689638566405898)
XLA Ops:
  0.6 145.1 %shampoo.1 = (f32[13,64,512]{2,1,0:T(8,128)}, f32[13,64,512]{2,1,0:T(8,128)}, f32[7,64,512]{2,1,0:T(8,128)}) custom-call(s32[224]{0:T(256)} %plan.1, bf16[7,512,512]{2,1,0:T(8,128)(2,1)} %bitcast.7, f32[13,64,512]{2,1,0:T(8,128)} %bitcast.8, f32[13,64,512]{2,1,0:T(8,128)} %bitcast.9, bf16[13,64,512]{2,1,0:T(8,128)(2,1)} %bitcast.12, ...), custom_call_target="tpu_custom_call" | custom-call | tf_op jit(solution)/shard_map/shampoo/pallas_call | solution.py:661
  145.7 0.0 copy-start
  145.7 2.9 %copy.12 = f32[1,13,64,512]{3,2,1,0:T(8,128)} copy(f32[1,13,64,512]{3,2,1,0:T(8,128)} %bitcast.11) | data formatting | bytes 3407872
  148.6 0.0 copy-done
  148.6 0.0 copy-start.1
  148.6 1.2 copy.13
  149.8 0.6 copy-done.1
  150.4 0.9 copy.14
Async XLA Ops:
  145.7 2.9 %copy-start = (f32[13,64,512]{2,1,0:T(8,128)S(1)}, f32[13,64,512]{2,1,0:T(8,128)}, u32[]{:S(2)}) copy-start(f32[13,64,512]{2,1,0:T(8,128)} %get-tuple-element.7) | copy-start | bytes 5111812
  148.6 1.8 %copy-start.1 = (f32[7,64,512]{2,1,0:T(8,128)S(1)}, f32[7,64,512]{2,1,0:T(8,128)}, u32[]{:S(2)}) copy-start(f32[7,64,512]{2,1,0:T(8,128)} %get-tuple-element.14) | copy-start | bytes 2752516

commit v4 on v3

v4 whole, which is shorter than its diff:
```python
import functools

import jax
import jax.numpy as jnp
from jax import lax
from jax.experimental import pallas as pl
from jax.experimental.pallas import tpu as pltpu
from jax.sharding import PartitionSpec as P

MESH = pl.DeviceIdType.MESH
f32 = jnp.float32
bf16 = jnp.bfloat16
i16 = jnp.int16
i32 = jnp.int32

stat_decay = 0.95
fresh_share = 0.05

NB = 7
NO = 32
NS = 13
ND = 8
SR = 64
BO = 512
CH = 128
NY = 4
NZ = 8
SLOT = 272
UNIT = 464
LIMIT = 60 * 1024 * 1024


def encode(x):
    m = jnp.maximum(jnp.max(jnp.abs(x), axis=0, keepdims=True), 2.0 ** -100)
    e = jnp.floor(jnp.log2(m) * 256.0) + 1.0
    q = jnp.round(x * (32700.0 * jnp.exp2(e * (-1.0 / 256.0))))
    return q.astype(i32).astype(i16), e


def scale_of(e16):
    return jnp.exp2(e16.astype(i32).astype(f32) * (1.0 / 256.0)) * (1.0 / 32700.0)


def widen(q):
    return q.astype(i32).astype(f32)


def remote(src, dst, send, recv, where):
    return pltpu.make_async_remote_copy(
        src_ref=src, dst_ref=dst, send_sem=send, recv_sem=recv,
        device_id=where, device_id_type=MESH)


def dot(a, b, dims=((1,), (0,))):
    return lax.dot_general(a, b, (dims, ((), ())), preferred_element_type=f32)


class Part:
    def __init__(self, p, chunks):
        w = len(chunks)
        self.p, self.chunks, self.w = p, chunks, w
        self.cols = slice(chunks[0] * CH, (chunks[-1] + 1) * CH)
        self.rows = SR * w
        self.unit = NB * SR * w + 16
        self.message = SR * w + 16
        self.front = slice(0, 4 * SR * w)
        self.rear = slice(4 * SR * w, self.unit)
        self.back = slice(4 * SR * w, NB * SR * w)
        self.scales = slice(NB * SR * w, self.unit)
        self.data = slice(0, SR * w)
        self.tail = slice(SR * w, self.message)


PARTS = (Part(0, (0,)), Part(1, (1, 2)), Part(2, (3,)))
NP = len(PARTS)


def split(v):
    hi = v.astype(bf16)
    return hi, (v - hi.astype(f32)).astype(bf16)


def rows_of(t, n=SR):
    return pl.ds(pl.multiple_of(t * n, n), n)


def shampoo_kernel(plan, grads, left_stat, right_stat, left_root, right_root,
                   left_new, right_new, update, *scratch):
    it = iter(scratch)
    slot_of, source_of, block_at, weight = (next(it) for _ in range(4))
    own, par, snd, rcv = (next(it) for _ in range(4))
    unit = [next(it) for _ in PARTS]
    hops = [[next(it) for _ in range(7)] for _ in PARTS]
    ysend, got, xs, gx = ([next(it) for _ in PARTS] for _ in range(4))
    lf, rf, ghi, glo, phi, plo = (next(it) for _ in range(6))
    xu, ux = ([next(it) for _ in PARTS] for _ in range(2))
    ybuf = [[next(it) for _ in range(8)] for _ in PARTS]
    yback = [next(it) for _ in PARTS]
    ur = [[next(it) for _ in range(4)] for _ in PARTS]
    dr = [[next(it) for _ in range(4)] for _ in PARTS]
    ush = [next(it) for _ in PARTS]
    dsh = [next(it) for _ in PARTS]
    sx, sr = ([next(it) for _ in range(2)] for _ in range(2))
    ls, rs = next(it), next(it)
    shelves = [next(it) for _ in PARTS]
    pair_sem, load_sem, unit_sem, line_sem, y_sem, x_sem, out_sem = (next(it) for _ in range(7))

    me = lax.axis_index("owner")
    z, y = me // NY, me % NY
    up, down = ((z + 1) % NZ) * NY + y, ((z + NZ - 1) % NZ) * NY + y
    dp = lax.axis_index("dp")
    x, c = dp // 2, dp % 2
    partner = x * 2 + 1 - c
    right = ((x + 1) % 4) * 2 + c
    left = ((x + 3) % 4) * 2 + c
    row_id = lax.broadcasted_iota(i32, (16, CH), 0)
    sent = []

    mine = {}
    for n, off in ((0, 2), (2, 3), (1, 1), (3, 0)):
        t = ((x + off) % 4) * 2 + c
        mine[n] = pltpu.make_async_copy(grads.at[:, rows_of(t), :], own.at[n], load_sem.at[n])
        mine[n].start()
    stat_in = [pltpu.make_async_copy(left_stat, ls, load_sem.at[4]),
               pltpu.make_async_copy(right_stat, rs, load_sem.at[5])]
    root_in = []
    for i in range(2):
        k = (dp + 8 * i) % NS
        root_in.append(pltpu.make_async_copy(
            left_root.at[k], lf.at[i, rows_of(dp)], load_sem.at[6 + i]))
        root_in.append(pltpu.make_async_copy(
            right_root.at[k], rf.at[i, rows_of(dp)], load_sem.at[8 + i]))

    barrier = pltpu.get_barrier_semaphore()
    for t in range(1, ND):
        pl.semaphore_signal(
            barrier, inc=1, device_id={"dp": (dp + t) % ND}, device_id_type=MESH)
    for place in [up, down] + [z * NY + (y + t) % NY for t in range(1, NY)]:
        pl.semaphore_signal(barrier, inc=1, device_id={"owner": place}, device_id_type=MESH)
    pl.semaphore_wait(barrier, ND - 1 + 2 + NY - 1)

    pair = {}
    for n, off in ((0, 2), (2, 3), (1, 1), (3, 0)):
        t = ((x + off) % 4) * 2 + 1 - c
        pair[n] = remote(grads.at[:, rows_of(t), :], par.at[n],
                         pair_sem.at[0, n], pair_sem.at[1, n], {"dp": partner})
        pair[n].start()
        sent.append(pair[n])
    for cp in root_in + stat_in:
        cp.start()

    def stand(i, count):
        hold, which = jnp.int32(0), jnp.int32(0)
        for j in range(NB):
            hit = (plan[i * NB + j] == me).astype(i32)
            hold = hold + hit * (1 - hold)
            which = which + hit * (j - which)
        slot_of[i] = count * (count < NS).astype(i32)
        source_of[NS + i] = hold * (count + 1) - 1
        block_at[NS + i] = which
        return count + hold

    count = lax.fori_loop(0, NO, stand, jnp.int32(0))

    def place_slots():
        def place(k, _):
            src, blk = jnp.int32(0), jnp.int32(0)
            for i in range(NO):
                hit = (source_of[NS + i] == k).astype(i32)
                src = src + hit * (i - src)
                blk = blk + hit * (block_at[NS + i] - blk)
            source_of[k] = src
            block_at[k] = blk
            weight[k] = fresh_share * (k < count).astype(i32).astype(f32)
            return 0

        lax.fori_loop(0, NS, place, 0)

    def pair_sum(n, j, k):
        cols = slice(k * CH, k * CH + CH)
        return own[n, j, :, cols].astype(f32) + par[n, j, :, cols].astype(f32)

    def scale_row(scales, r):
        return jnp.sum(jnp.where(row_id == r, scales, 0.0), axis=0, keepdims=True)

    def received(u, j):
        scales = scale_of(rcv[u, NB * SR:UNIT, :])
        return widen(rcv[u, j * SR:j * SR + SR, :]) * scales[j:j + 1, :]

    def fill(out, w, value):
        sc = jnp.zeros((16, CH), f32)
        for j in range(NB):
            for kk in range(w):
                r = j * w + kk
                q, e = encode(value(j, kk))
                out[r * SR:r * SR + SR, :] = q
                sc = jnp.where(row_id == r, e, sc)
        out[NB * SR * w:NB * SR * w + 16, :] = sc.astype(i32).astype(i16)

    def ship(u, to):
        cp = remote(snd.at[u], rcv.at[u], unit_sem.at[0, u], unit_sem.at[1, u], {"dp": to})
        cp.start()
        sent.append(cp)
        return cp

    def ready(n):
        mine[n].wait()
        pair[n].wait_recv()

    class Line:
        def __init__(self, p, way, towards):
            self.p, self.way, self.towards = p, way, towards
            self.copies = {}

        def go(self, n, src, dst):
            cp = remote(src, dst, line_sem.at[self.p, self.way, 0, n],
                        line_sem.at[self.p, self.way, 1, n], {"owner": self.towards})
            cp.start()
            sent.append(cp)
            self.copies[n] = cp

        def came(self, *names):
            for n in names:
                self.copies[n].wait_recv()

    class Outward:
        def __init__(self, part):
            self.part, self.p = part, part.p
            self.u1, self.u2, self.u3, self.d1, self.d2, self.d3, self.far = hops[part.p]
            self.ups, self.downs = Line(part.p, 0, up), Line(part.p, 1, down)
            self.hand, self.given = [], []

        def pass_on(self, n, ref, rel):
            part, p = self.part, self.p
            shelf = shelves[p]
            src = ((z + rel) % NZ) * NY + y

            def code(yy):
                j = jnp.int32(0)
                for b in range(NB):
                    j = j + (plan[src * NB + b] == z * NY + yy).astype(i32) * (b - j)
                return shelf[j]

            for b in range(NB):
                shelf[b] = ref[b * part.rows:(b + 1) * part.rows, :]
            scales = ref[part.scales, :]
            for t in range(1, NY):
                yy = (y + t) % NY
                ysend[p][n, t - 1, part.data, :] = code(yy)
                ysend[p][n, t - 1, part.tail, :] = scales
                cp = remote(ysend[p].at[n, t - 1], got[p].at[src], y_sem.at[p, 0, n, t - 1],
                            y_sem.at[p, 1, n, t - 1], {"owner": z * NY + yy})
                cp.start()
                sent.append(cp)
                self.hand.append(cp)
            got[p][src, part.data, :] = code(y)
            got[p][src, part.tail, :] = scales

        def start(self):
            front, rear = self.part.front, self.part.rear
            g = unit[self.p]
            self.ups.go(0, g.at[front], self.u1.at[front])
            self.downs.go(0, g.at[rear], self.d1.at[rear])
            self.ups.go(1, g.at[rear], self.u1.at[rear])
            self.downs.go(1, g.at[front], self.d1.at[front])
            self.pass_on(0, g, 0)

        def step(self, r):
            ups, downs = self.ups, self.downs
            front, rear = self.part.front, self.part.rear
            if r < 3:
                ua, ub = ((self.u1, self.u2), (self.u2, self.u3))[r - 1]
                da, db = ((self.d1, self.d2), (self.d2, self.d3))[r - 1]
                ups.came(2 * r - 2)
                ups.go(2 * r, ua.at[front], ub.at[front])
                downs.came(2 * r - 2)
                downs.go(2 * r, da.at[rear], db.at[rear])
                ups.came(2 * r - 1)
                ups.go(2 * r + 1, ua.at[rear], ub.at[rear])
                downs.came(2 * r - 1)
                downs.go(2 * r + 1, da.at[front], db.at[front])
                self.pass_on(2 * r - 1, ua, NZ - r)
                self.pass_on(2 * r, da, r)
            else:
                ups.came(4)
                ups.go(6, self.u3.at[front], self.far.at[front])
                downs.came(4)
                downs.go(6, self.d3.at[rear], self.far.at[rear])
                ups.came(5)
                downs.came(5)
                self.pass_on(5, self.u3, 5)
                self.pass_on(6, self.d3, 3)

        def last(self):
            self.ups.came(6)
            self.downs.came(6)
            self.pass_on(7, self.far, 4)

        def spread(self):
            p = self.p
            for cp in self.hand:
                cp.wait_recv()
            for t in (4, 3, 5, 2, 6, 1, 7, 0):
                for i in range(2):
                    to = (dp + t) % ND
                    k = (to + 8 * i) % NS
                    if t == 0:
                        gx[p][i, dp] = got[p][source_of[k]]
                        continue
                    xs[p][i, t] = got[p][source_of[k]]
                    cp = remote(xs[p].at[i, t], gx[p].at[i, dp], x_sem.at[p, 0, i, t],
                                x_sem.at[p, 1, i, t], {"dp": to})
                    cp.start()
                    sent.append(cp)
                    self.given.append(cp)

        def open(self):
            part, p = self.part, self.p
            for cp in self.given:
                cp.wait_recv()
            for i in range(2):
                blk = block_at[(dp + 8 * i) % NS]
                for t in range(ND):
                    scales = scale_of(gx[p][i, t, part.tail, :])
                    for kk, n in enumerate(part.chunks):
                        v = (widen(gx[p][i, t, kk * SR:kk * SR + SR, :])
                             * scale_row(scales, blk * part.w + kk))
                        hi, lo = split(v)
                        ghi[i, t * SR:t * SR + SR, n * CH:n * CH + CH] = hi
                        glo[i, t * SR:t * SR + SR, n * CH:n * CH + CH] = lo

        def project(self):
            cols = self.part.cols

            def part(m, _):
                i, rows = m // 2, rows_of(m % 2, 256)
                p = dot(lf[i, rows, :], ghi[i, :, cols]) + dot(lf[i, rows, :], glo[i, :, cols])
                hi, lo = split(p)
                phi[i, rows, cols] = hi
                plo[i, rows, cols] = lo
                return 0

            lax.fori_loop(0, 4, part, 0, unroll=True)

    class Train:
        def __init__(self, part, way, towards, land, out, ascending):
            self.part, self.p, self.land, self.out = part, part.p, land, out
            self.ascending = ascending
            self.line = Line(part.p, way, towards)

        def place(self, r):
            return r if self.ascending else NZ - r

        def blocks(self, r, front, came):
            p, part, out = self.p, self.part, self.out
            src = ((z + self.place(r)) % NZ) * NY + y
            first, last, cut = (0, 4, part.front) if front else (4, NB, part.back)
            for j in range(first, last):
                rows = slice(j * part.rows, (j + 1) * part.rows)
                o = plan[src * NB + j]
                new = ybuf[p][self.place(r)][lax.rem(o, NY)][part.data, :]
                if came is not None:
                    at = jnp.full((part.rows, CH), (lax.div(o, NY) == z).astype(i32), i32)
                    new = jnp.where(at > 0, new.astype(i32), came[rows, :].astype(i32)).astype(i16)
                out[r - 1, rows, :] = new
            return out.at[r - 1, cut], self.land[r - 1].at[cut]

        def scales(self, r, came):
            p, part, out = self.p, self.part, self.out
            src = ((z + self.place(r)) % NZ) * NY + y
            tile = jnp.zeros((16, CH), i32) if came is None else came[part.scales, :].astype(i32)
            for j in range(NB):
                o = plan[src * NB + j]
                new = ybuf[p][self.place(r)][lax.rem(o, NY)][part.tail, :].astype(i32)
                at = (row_id // part.w == j).astype(i32) * (lax.div(o, NY) == z).astype(i32)
                tile = jnp.where(at > 0, new, tile)
            out[r - 1, part.scales, :] = tile.astype(i16)
            return out.at[r - 1, part.scales], self.land[r - 1].at[part.scales]

        def head(self, r):
            came = None
            if r < 3:
                self.line.came(2 * (2 - r) + 1)
                came = self.land[r]
            self.line.go(2 * (3 - r) + 1, *self.blocks(r, not self.ascending, came))

        def tail(self, r):
            came = None
            if r < 4:
                self.line.came(2 * (2 - r) + 2, 10 - r)
                came = self.land[r]
            self.line.go(2 * (3 - r) + 2, *self.blocks(r, self.ascending, came))
            self.line.go(11 - r, *self.scales(r, came))

        def arrived(self):
            self.line.came(5, 6, 10)

    class Inward:
        def __init__(self, part):
            self.part, self.p = part, part.p
            self.ups = Train(part, 2, up, ur[part.p], ush[part.p], True)
            self.downs = Train(part, 3, down, dr[part.p], dsh[part.p], False)
            self.hand, self.given = {}, []

        def multiply(self, i):
            part, p = self.part, self.p

            def pairs(m, _):
                b = (x + 2 + m) % 4
                rows = rows_of(b, 128)
                r = dot(jnp.concatenate((phi[i, rows, :], plo[i, rows, :]), axis=0),
                        rf[i, :, part.cols])
                u = r[:128] + r[128:]
                for cc in range(2):
                    sc = jnp.zeros((16, CH), f32)
                    for kk in range(part.w):
                        q, e = encode(u[cc * SR:cc * SR + SR, kk * CH:kk * CH + CH])
                        xu[p][i, b * 2 + cc, kk * SR:kk * SR + SR, :] = q
                        sc = jnp.where(row_id % part.w == kk, e, sc)
                    xu[p][i, b * 2 + cc, part.tail, :] = sc.astype(i32).astype(i16)
                return 0

            lax.fori_loop(0, 4, pairs, 0, unroll=True)

        def hand_out(self, i):
            p = self.p
            ux[p][dp + 8 * i] = xu[p][i, dp]
            for t in (4, 3, 5, 2, 6, 1, 7):
                to = (dp + t) % ND
                cp = remote(xu[p].at[i, to], ux[p].at[dp + 8 * i], x_sem.at[NP + p, 0, i, t],
                            x_sem.at[NP + p, 1, i, t], {"dp": to})
                cp.start()
                sent.append(cp)
                self.given.append(cp)

        def arrive(self):
            for cp in self.given:
                cp.wait_recv()

        def across(self, n):
            p = self.p
            d = (z + n) % NZ
            self.hand[n] = []
            for t in range(1, NY):
                yy = (y + t) % NY
                yback[p][n, t - 1] = ux[p][slot_of[d * NY + yy]]
                cp = remote(yback[p].at[n, t - 1], ybuf[p][n].at[y],
                            y_sem.at[NP + p, 0, n, t - 1], y_sem.at[NP + p, 1, n, t - 1],
                            {"owner": z * NY + yy})
                cp.start()
                sent.append(cp)
                self.hand[n].append(cp)
            ybuf[p][n][y] = ux[p][slot_of[d * NY + y]]

        def crossed(self, n):
            for cp in self.hand[n]:
                cp.wait_recv()

        def begin(self):
            self.across(4)
            self.across(3)
            self.across(5)

        def one(self):
            self.crossed(4)
            self.ups.tail(4)
            self.downs.tail(4)
            self.crossed(3)
            self.ups.head(3)
            self.crossed(5)
            self.downs.head(3)
            self.across(2)
            self.across(6)

        def two(self):
            self.ups.tail(3)
            self.downs.tail(3)
            self.across(1)
            self.across(7)
            self.crossed(2)
            self.ups.head(2)
            self.crossed(6)
            self.downs.head(2)

        def three(self):
            self.ups.tail(2)
            self.downs.tail(2)
            self.across(0)
            self.crossed(1)
            self.ups.head(1)
            self.crossed(7)
            self.downs.head(1)

        def four(self):
            self.ups.tail(1)
            self.downs.tail(1)

        def finish(self):
            part, p = self.part, self.p
            self.crossed(0)
            self.ups.arrived()
            self.downs.arrived()
            for j in range(NB):
                o = plan[me * NB + j]
                near = ybuf[p][0][lax.rem(o, NY)].astype(i32)
                off = lax.rem(lax.div(o, NY) + NZ - z, NZ)
                above = (off < 4).astype(i32)
                if j >= 4:
                    above = above + (off == 4).astype(i32)
                local = (off == 0).astype(i32)
                rows = slice(j * part.rows, (j + 1) * part.rows)
                full = jnp.zeros((part.rows, CH), i32)
                code = jnp.where(full + above > 0, dr[p][0][rows, :].astype(i32),
                                 ur[p][0][rows, :].astype(i32))
                code = jnp.where(full + local > 0, near[part.data, :], code)
                tile = jnp.where(row_id * 0 + above > 0, dr[p][0][part.scales, :].astype(i32),
                                 ur[p][0][part.scales, :].astype(i32))
                tile = jnp.where(row_id * 0 + local > 0, near[part.tail, :], tile)
                tile = scale_of(tile)
                for kk, n in enumerate(part.chunks):
                    r = j * part.w + kk
                    update[j, :, n * CH:n * CH + CH] = (
                        code[kk * SR:kk * SR + SR].astype(f32) * tile[r:r + 1, :])

    stat_came = [[], []]

    def stat(which, i):
        def block(m, _):
            b = (x + 1 + m) % 4
            if which == 0:
                ohi, olo = ghi[i, rows_of(b, 128), :], glo[i, rows_of(b, 128), :]
                f = dot(jnp.concatenate((ohi, olo), axis=0), ghi[i], ((1,), (1,)))
                f = f[:128] + f[128:] + dot(ohi, glo[i], ((1,), (1,)))
            else:
                chi, clo = ghi[i, :, rows_of(b, 128)], glo[i, :, rows_of(b, 128)]
                f = (dot(chi, ghi[i], ((0,), (0,))) + dot(clo, ghi[i], ((0,), (0,)))
                     + dot(chi, glo[i], ((0,), (0,))))
            for cc in range(2):
                sc = jnp.zeros((16, CH), f32)
                for n in range(4):
                    q, e = encode(f[cc * SR:cc * SR + SR, n * CH:n * CH + CH])
                    sx[which][i, b * 2 + cc, n * SR:n * SR + SR, :] = q
                    sc = jnp.where(row_id == n, e, sc)
                sx[which][i, b * 2 + cc, 256:SLOT, :] = sc.astype(i32).astype(i16)
            return 0

        lax.fori_loop(0, 4, block, 0, unroll=2)
        sr[which][dp + 8 * i] = sx[which][i, dp]
        for t in (4, 3, 5, 2, 6, 1, 7):
            to = (dp + t) % ND
            cp = remote(sx[which].at[i, to], sr[which].at[dp + 8 * i], x_sem.at[2 * NP + which, 0, i, t],
                        x_sem.at[2 * NP + which, 1, i, t], {"dp": to})
            cp.start()
            sent.append(cp)
            stat_came[which].append(cp)

    def renew(which, held, out):
        for cp in stat_came[which]:
            cp.wait_recv()

        def slot(k, _):
            w = weight[k]
            scales = scale_of(sr[which][k, 256:SLOT, :])
            for n in range(4):
                cols = slice(n * CH, n * CH + CH)
                term = widen(sr[which][k, n * SR:n * SR + SR, :]) * scales[n:n + 1, :]
                held[k, :, cols] = stat_decay * held[k, :, cols] + w * term
            pltpu.make_async_copy(held.at[k], out.at[k], out_sem.at[which, k]).start()
            return 0

        lax.fori_loop(0, NS, slot, 0)

    out0, out1, out2 = (Outward(part) for part in PARTS)
    in0, in1, in2 = (Inward(part) for part in PARTS)
    right_far, left_far, right_straight, left_straight, right_both, left_both = {}, {}, {}, {}, {}, {}

    def far(k):
        fill(snd.at[k], 1, lambda j, kk: pair_sum(0, j, k))
        if k < 2:
            right_far[k] = ship(k, right)
        else:
            left_far[k] = ship(k, left)

    def straight(k):
        if k >= 2:
            fill(snd.at[4 + k], 1, lambda j, kk: pair_sum(1, j, k))
            right_straight[k] = ship(4 + k, right)
        else:
            fill(snd.at[4 + k], 1, lambda j, kk: pair_sum(2, j, k))
            left_straight[k] = ship(4 + k, left)

    def both(k):
        if k < 2:
            right_far[k].wait_recv()
            fill(snd.at[8 + k], 1, lambda j, kk: pair_sum(1, j, k) + received(k, j))
            right_both[k] = ship(8 + k, right)
        else:
            left_far[k].wait_recv()
            fill(snd.at[8 + k], 1, lambda j, kk: pair_sum(2, j, k) + received(k, j))
            left_both[k] = ship(8 + k, left)

    def total(part):
        for k in part.chunks:
            for cps in (right_straight, left_straight, right_both, left_both):
                if k in cps:
                    cps[k].wait_recv()
        fill(unit[part.p], part.w, lambda j, kk: (
            pair_sum(3, j, part.chunks[kk]) + received(4 + part.chunks[kk], j)
            + received(8 + part.chunks[kk], j)))

    ready(0)
    far(0)
    far(1)
    ready(2)
    straight(0)
    far(2)
    far(3)
    ready(1)
    both(0)
    straight(1)
    both(1)
    straight(2)
    straight(3)
    ready(3)
    total(PARTS[0])
    out0.start()
    both(2)
    both(3)
    out0.step(1)
    total(PARTS[1])
    out1.start()
    out0.step(2)
    total(PARTS[2])
    roots = []
    for which, (src, dst) in enumerate(((left_root, lf), (right_root, rf))):
        for i in range(2):
            for t in range(1, ND):
                to = (dp + t) % ND
                cp = remote(src.at[(to + 8 * i) % NS], dst.at[i, rows_of(dp)],
                            x_sem.at[2 * NP + 2 + which, 0, i, t],
                            x_sem.at[2 * NP + 2 + which, 1, i, t], {"dp": to})
                cp.start()
                sent.append(cp)
                roots.append(cp)
    out0.step(3)
    out1.step(1)
    place_slots()
    out0.last()
    out1.step(2)
    out0.spread()
    out1.step(3)
    out2.start()
    out0.open()
    out1.last()
    out2.step(1)
    out1.spread()
    out2.step(2)
    for cp in root_in:
        cp.wait()
    for cp in roots:
        cp.wait_recv()
    out0.project()
    out2.step(3)
    out1.open()
    out1.project()
    out2.last()
    out2.spread()
    out2.open()
    out2.project()
    in0.multiply(0)
    in0.hand_out(0)
    in0.multiply(1)
    in0.hand_out(1)
    in1.multiply(0)
    in1.multiply(1)
    in0.arrive()
    in0.begin()
    in1.hand_out(0)
    in1.hand_out(1)
    in0.one()
    in2.multiply(0)
    in2.multiply(1)
    in0.two()
    in1.arrive()
    in1.begin()
    in2.hand_out(0)
    in2.hand_out(1)
    in1.one()
    in0.three()
    stat(0, 0)
    in0.four()
    in1.two()
    stat(1, 0)
    in2.arrive()
    in2.begin()
    in1.three()
    in2.one()
    stat(0, 1)
    in1.four()
    in0.finish()
    in2.two()
    stat(1, 1)
    in2.three()
    for cp in stat_in:
        cp.wait()
    in1.finish()
    in2.four()
    renew(0, ls, left_new)
    renew(1, rs, right_new)
    in2.finish()

    def done(k, _):
        pltpu.make_async_copy(ls.at[k], left_new.at[k], out_sem.at[0, k]).wait()
        pltpu.make_async_copy(rs.at[k], right_new.at[k], out_sem.at[1, k]).wait()
        return 0

    lax.fori_loop(0, NS, done, 0)
    for cp in sent:
        cp.wait_send()


def shampoo(plan, grads, left_stat, right_stat, left_root, right_root):
    hbm = pl.BlockSpec(memory_space=pl.ANY)
    vmem = pltpu.VMEM

    def each(lead, rows, times=1):
        return [vmem((*lead, rows(part), CH), i16) for part in PARTS for _ in range(times)]

    def unit(part):
        return part.unit

    def message(part):
        return part.message

    return pl.pallas_call(
        shampoo_kernel,
        out_shape=(
            jax.ShapeDtypeStruct((NS, SR, BO), f32),
            jax.ShapeDtypeStruct((NS, SR, BO), f32),
            jax.ShapeDtypeStruct((NB, SR, BO), f32),
        ),
        in_specs=[pl.BlockSpec(memory_space=pltpu.SMEM), hbm, hbm, hbm, hbm, hbm],
        out_specs=(hbm, hbm, pl.BlockSpec(memory_space=vmem)),
        scratch_shapes=[
            pltpu.SMEM((NO,), i32),
            pltpu.SMEM((NS + NO,), i32),
            pltpu.SMEM((NS + NO,), i32),
            pltpu.SMEM((NS,), f32),
            vmem((4, NB, SR, BO), bf16),
            vmem((4, NB, SR, BO), bf16),
            vmem((12, UNIT, CH), i16),
            vmem((12, UNIT, CH), i16),
            *each((), unit),
            *each((), unit, 7),
            *each((NZ, NY - 1), message),
            *each((NO,), message),
            *each((2, ND), message),
            *each((2, ND), message),
            *[vmem((2, BO, BO), bf16)] * 6,
            *each((2, ND), message),
            *each((2 * ND,), message),
            *each((NY,), message, NZ),
            *each((NZ, NY - 1), message),
            *each((), unit, 4),
            *each((), unit, 4),
            *each((4,), unit),
            *each((4,), unit),
            *[vmem((2, ND, SLOT, CH), i16)] * 2,
            *[vmem((2 * ND, SLOT, CH), i16)] * 2,
            vmem((NS, SR, BO), f32),
            vmem((NS, SR, BO), f32),
            *[vmem((NB, part.rows, CH), i16) for part in PARTS],
            pltpu.SemaphoreType.DMA((2, 4)),
            pltpu.SemaphoreType.DMA((10,)),
            pltpu.SemaphoreType.DMA((2, 12)),
            pltpu.SemaphoreType.DMA((NP, 4, 2, 11)),
            pltpu.SemaphoreType.DMA((2 * NP, 2, NZ, NY - 1)),
            pltpu.SemaphoreType.DMA((2 * NP + 4, 2, 2, ND)),
            pltpu.SemaphoreType.DMA((2, NS)),
        ],
        compiler_params=pltpu.CompilerParams(
            collective_id=0, has_side_effects=True, vmem_limit_bytes=LIMIT),
        name="shampoo",
    )(plan, grads, left_stat, right_stat, left_root, right_root)


def local(grads, plan, left_stat, right_stat, left_root, right_root):
    left_new, right_new, update = shampoo(
        plan, grads[0], left_stat[0], right_stat[0], left_root[0], right_root[0])
    return left_new[None], right_new[None], update


def solution(mesh):
    return jax.shard_map(
        local,
        mesh=mesh,
        in_specs=(
            P("dp", "owner", None, None),
            P(),
            P("owner", None, "dp", None),
            P("owner", None, "dp", None),
            P("owner", None, "dp", None),
            P("owner", None, "dp", None),
        ),
        out_specs=(
            P("owner", None, "dp", None),
            P("owner", None, "dp", None),
            P("owner", "dp", None),
        ),
        check_vma=False,
    )
```

time: 152 us -> 154 us (1.013)
  no operation moved by 1% of the time
where the time goes in v4:
time: 154 us; the launch traced here: 152 us
  Pallas kernels  146 us (95%)
  local copies, waits for them, and re-layouts  5.62 us (4%)
    pallas_call x1, Pallas kernels, shampoo(): pl.pallas_call(shampoo_kernel, out_shape=(jax.ShapeDtypeStruct((NS, SR, B...  146 us
    unnamed x7, local copies, waits for them, and re-layouts  5.62 us

profile of v4, /device:TPU:8, one launch (start us, length us, event | category | flops | bytes accessed | tf_op | source)
XLA Modules:
  0.0 152.4 jit_solution(12128562266109848570)
XLA Ops:
  0.6 146.1 %shampoo.1 = (f32[13,64,512]{2,1,0:T(8,128)}, f32[13,64,512]{2,1,0:T(8,128)}, f32[7,64,512]{2,1,0:T(8,128)}) custom-call(s32[224]{0:T(256)} %plan.1, bf16[7,512,512]{2,1,0:T(8,128)(2,1)} %bitcast.7, f32[13,64,512]{2,1,0:T(8,128)} %bitcast.8, f32[13,64,512]{2,1,0:T(8,128)} %bitcast.9, bf16[13,64,512]{2,1,0:T(8,128)(2,1)} %bitcast.12, ...), custom_call_target="tpu_custom_call" | custom-call | tf_op jit(solution)/shard_map/shampoo/pallas_call | solution.py:735
  146.8 0.0 copy-start
  146.8 2.9 %copy.12 = f32[1,13,64,512]{3,2,1,0:T(8,128)} copy(f32[1,13,64,512]{3,2,1,0:T(8,128)} %bitcast.11) | data formatting | bytes 3407872
  149.7 0.0 copy-done
  149.7 0.0 copy-start.1
  149.7 1.2 copy.13
  150.9 0.6 copy-done.1
  151.5 0.9 copy.14
Async XLA Ops:
  146.8 2.9 %copy-start = (f32[13,64,512]{2,1,0:T(8,128)S(1)}, f32[13,64,512]{2,1,0:T(8,128)}, u32[]{:S(2)}) copy-start(f32[13,64,512]{2,1,0:T(8,128)} %get-tuple-element.7) | copy-start | bytes 5111812
  149.7 1.8 %copy-start.1 = (f32[7,64,512]{2,1,0:T(8,128)S(1)}, f32[7,64,512]{2,1,0:T(8,128)}, u32[]{:S(2)}) copy-start(f32[7,64,512]{2,1,0:T(8,128)} %get-tuple-element.14) | copy-start | bytes 2752516

commit v5 on v4

--- a/solution.py
+++ b/solution.py
@@ -69,6 +69,8 @@
         self.scales = slice(NB * SR * w, self.unit)
         self.data = slice(0, SR * w)
         self.tail = slice(SR * w, self.message)
+        self.far = 2 * SR * w + 16
+        self.six = 6 * SR * w + 16
 
 
 PARTS = (Part(0, (0,)), Part(1, (1, 2)), Part(2, (3,)))
@@ -90,20 +92,19 @@
     slot_of, source_of, block_at, weight = (next(it) for _ in range(4))
     own, par, snd, rcv = (next(it) for _ in range(4))
     unit = [next(it) for _ in PARTS]
-    hops = [[next(it) for _ in range(7)] for _ in PARTS]
+    hops = [[next(it) for _ in range(9)] for _ in PARTS]
     ysend, got, xs, gx = ([next(it) for _ in PARTS] for _ in range(4))
     lf, rf, ghi, glo, phi, plo = (next(it) for _ in range(6))
     xu, ux = ([next(it) for _ in PARTS] for _ in range(2))
     ybuf = [[next(it) for _ in range(8)] for _ in PARTS]
     yback = [next(it) for _ in PARTS]
-    ur = [[next(it) for _ in range(4)] for _ in PARTS]
-    dr = [[next(it) for _ in range(4)] for _ in PARTS]
-    ush = [next(it) for _ in PARTS]
-    dsh = [next(it) for _ in PARTS]
+    ur = [[next(it) for _ in range(7)] for _ in PARTS]
+    dr = [[next(it) for _ in range(7)] for _ in PARTS]
     sx, sr = ([next(it) for _ in range(2)] for _ in range(2))
     ls, rs = next(it), next(it)
     shelves = [next(it) for _ in PARTS]
-    pair_sem, load_sem, unit_sem, line_sem, y_sem, x_sem, out_sem = (next(it) for _ in range(7))
+    pair_sem, load_sem, unit_sem, line_sem, y_sem, back_sem, x_sem, out_sem = (
+        next(it) for _ in range(8))
 
     me = lax.axis_index("owner")
     z, y = me // NY, me % NY
@@ -115,6 +116,12 @@
     left = ((x + 3) % 4) * 2 + c
     row_id = lax.broadcasted_iota(i32, (16, CH), 0)
     sent = []
+    group = []
+
+    def whole(ref, sems):
+        cp = remote(ref, ref, sems.at[0], sems.at[1], {"dp": partner})
+        group.append(cp)
+        return cp
 
     mine = {}
     for n, off in ((0, 2), (2, 3), (1, 1), (3, 0)):
@@ -152,26 +159,26 @@
     def stand(i, count):
         hold, which = jnp.int32(0), jnp.int32(0)
         for j in range(NB):
-            hit = (plan[i * NB + j] == me).astype(i32)
-            hold = hold + hit * (1 - hold)
-            which = which + hit * (j - which)
-        slot_of[i] = count * (count < NS).astype(i32)
-        source_of[NS + i] = hold * (count + 1) - 1
+            hit = plan[i * NB + j] == me
+            hold = jnp.where(hit, 1, hold)
+            which = jnp.where(hit, j, which)
+        slot_of[i] = jnp.minimum(count, NS - 1)
+        source_of[NS + i] = jnp.where(hold > 0, count, -1)
         block_at[NS + i] = which
         return count + hold
 
-    count = lax.fori_loop(0, NO, stand, jnp.int32(0))
-
     def place_slots():
+        count = lax.fori_loop(0, NO, stand, jnp.int32(0))
+
         def place(k, _):
             src, blk = jnp.int32(0), jnp.int32(0)
             for i in range(NO):
-                hit = (source_of[NS + i] == k).astype(i32)
-                src = src + hit * (i - src)
-                blk = blk + hit * (block_at[NS + i] - blk)
+                hit = source_of[NS + i] == k
+                src = jnp.where(hit, i, src)
+                blk = jnp.where(hit, block_at[NS + i], blk)
             source_of[k] = src
             block_at[k] = blk
-            weight[k] = fresh_share * (k < count).astype(i32).astype(f32)
+            weight[k] = jnp.where(k < count, fresh_share, 0.0).astype(f32)
             return 0
 
         lax.fori_loop(0, NS, place, 0)
@@ -226,35 +233,49 @@
     class Outward:
         def __init__(self, part):
             self.part, self.p = part, part.p
-            self.u1, self.u2, self.u3, self.d1, self.d2, self.d3, self.far = hops[part.p]
+            (self.u1, self.u2, self.d1, self.d2, self.u3, self.d3, self.far,
+             self.su, self.sd) = hops[part.p]
             self.ups, self.downs = Line(part.p, 0, up), Line(part.p, 1, down)
-            self.hand, self.given = [], []
-
-        def pass_on(self, n, ref, rel):
+
+        def shelve(self, ref):
+            shelf = shelves[self.p]
+            for b in range(NB):
+                shelf[b] = ref[b * self.part.rows:(b + 1) * self.part.rows, :]
+
+        def find(self, src, owner):
+            j = jnp.int32(0)
+            for b in range(NB):
+                j = jnp.where(plan[src * NB + b] == owner, b, j)
+            return shelves[self.p][j]
+
+        def hand(self, n, src, code, scales):
             part, p = self.part, self.p
-            shelf = shelves[p]
-            src = ((z + rel) % NZ) * NY + y
-
-            def code(yy):
-                j = jnp.int32(0)
-                for b in range(NB):
-                    j = j + (plan[src * NB + b] == z * NY + yy).astype(i32) * (b - j)
-                return shelf[j]
-
-            for b in range(NB):
-                shelf[b] = ref[b * part.rows:(b + 1) * part.rows, :]
-            scales = ref[part.scales, :]
             for t in range(1, NY):
                 yy = (y + t) % NY
                 ysend[p][n, t - 1, part.data, :] = code(yy)
-                ysend[p][n, t - 1, part.tail, :] = scales
-                cp = remote(ysend[p].at[n, t - 1], got[p].at[src], y_sem.at[p, 0, n, t - 1],
-                            y_sem.at[p, 1, n, t - 1], {"owner": z * NY + yy})
-                cp.start()
-                sent.append(cp)
-                self.hand.append(cp)
+                ysend[p][n, t - 1, part.tail, :] = scales(yy)
+                remote(ysend[p].at[n, t - 1], got[p].at[src], y_sem.at[p, 0],
+                       y_sem.at[p, 1], {"owner": z * NY + yy}).start()
             got[p][src, part.data, :] = code(y)
-            got[p][src, part.tail, :] = scales
+            got[p][src, part.tail, :] = scales(y)
+
+        def pass_on(self, n, ref, rel):
+            src = ((z + rel) % NZ) * NY + y
+            self.shelve(ref)
+            scales = ref[self.part.scales, :]
+            self.hand(n, src, lambda yy: self.find(src, z * NY + yy), lambda yy: scales)
+
+        def pack(self, out, ref, rel, way, first):
+            rows = self.part.rows
+            src = ((z + rel) % NZ) * NY + y
+            self.shelve(ref)
+            one, two = ((z + way) % NZ) * NY, ((z + 2 * way) % NZ) * NY
+            for q in range(2):
+                out[q * rows:q * rows + rows, :] = self.find(src, two + first + q)
+            out[2 * rows:2 * rows + 16, :] = ref[self.part.scales, :]
+            for q in range(NY):
+                at = self.part.far + q * rows
+                out[at:at + rows, :] = self.find(src, one + q)
 
         def start(self):
             front, rear = self.part.front, self.part.rear
@@ -268,38 +289,62 @@
         def step(self, r):
             ups, downs = self.ups, self.downs
             front, rear = self.part.front, self.part.rear
-            if r < 3:
-                ua, ub = ((self.u1, self.u2), (self.u2, self.u3))[r - 1]
-                da, db = ((self.d1, self.d2), (self.d2, self.d3))[r - 1]
-                ups.came(2 * r - 2)
-                ups.go(2 * r, ua.at[front], ub.at[front])
-                downs.came(2 * r - 2)
-                downs.go(2 * r, da.at[rear], db.at[rear])
-                ups.came(2 * r - 1)
-                ups.go(2 * r + 1, ua.at[rear], ub.at[rear])
-                downs.came(2 * r - 1)
-                downs.go(2 * r + 1, da.at[front], db.at[front])
-                self.pass_on(2 * r - 1, ua, NZ - r)
-                self.pass_on(2 * r, da, r)
+            far, six, rows = self.part.far, self.part.six, self.part.rows
+            if r == 1:
+                ups.came(0)
+                ups.go(2, self.u1.at[front], self.u2.at[front])
+                downs.came(0)
+                downs.go(2, self.d1.at[rear], self.d2.at[rear])
+                ups.came(1)
+                ups.go(3, self.u1.at[rear], self.u2.at[rear])
+                downs.came(1)
+                downs.go(3, self.d1.at[front], self.d2.at[front])
+                self.pass_on(1, self.u1, 7)
+                self.pass_on(2, self.d1, 1)
+            elif r == 2:
+                ups.came(2, 3)
+                self.pack(self.su, self.u2, 6, 1, 0)
+                ups.go(4, self.su.at[0:far], self.u3.at[0:far])
+                ups.go(5, self.su.at[far:six], self.u3.at[far:six])
+                downs.came(2, 3)
+                self.pack(self.sd, self.d2, 2, NZ - 1, 2)
+                downs.go(4, self.sd.at[0:far], self.d3.at[0:far])
+                downs.go(5, self.sd.at[far:six], self.d3.at[far:six])
+                self.pass_on(3, self.u2, 6)
+                self.pass_on(4, self.d2, 2)
             else:
                 ups.came(4)
-                ups.go(6, self.u3.at[front], self.far.at[front])
+                ups.go(6, self.u3.at[0:far], self.far.at[0:far])
                 downs.came(4)
-                downs.go(6, self.d3.at[rear], self.far.at[rear])
-                ups.came(5)
-                downs.came(5)
-                self.pass_on(5, self.u3, 5)
-                self.pass_on(6, self.d3, 3)
+                downs.go(6, self.d3.at[0:far], self.far.at[far:2 * far])
+                for line, ref, n, rel in ((ups, self.u3, 5, 5), (downs, self.d3, 6, 3)):
+                    line.came(5)
+
+                    def code(yy, ref=ref):
+                        return ref[pl.ds(pl.multiple_of(far + yy * rows, 16), rows), :]
+
+                    def scales(yy, ref=ref):
+                        return ref[2 * rows:far, :]
+
+                    self.hand(n, ((z + rel) % NZ) * NY + y, code, scales)
 
         def last(self):
+            far, rows = self.part.far, self.part.rows
             self.ups.came(6)
             self.downs.came(6)
-            self.pass_on(7, self.far, 4)
+
+            def code(yy):
+                at = (yy // 2) * far + (yy % 2) * rows
+                return self.far[pl.ds(pl.multiple_of(at, 16), rows), :]
+
+            def scales(yy):
+                return self.far[pl.ds(pl.multiple_of((yy // 2) * far + 2 * rows, 16), 16), :]
+
+            self.hand(7, ((z + 4) % NZ) * NY + y, code, scales)
 
         def spread(self):
             p = self.p
-            for cp in self.hand:
-                cp.wait_recv()
+            whole(ysend[p], y_sem.at[p]).wait_recv()
             for t in (4, 3, 5, 2, 6, 1, 7, 0):
                 for i in range(2):
                     to = (dp + t) % ND
@@ -308,16 +353,12 @@
                         gx[p][i, dp] = got[p][source_of[k]]
                         continue
                     xs[p][i, t] = got[p][source_of[k]]
-                    cp = remote(xs[p].at[i, t], gx[p].at[i, dp], x_sem.at[p, 0, i, t],
-                                x_sem.at[p, 1, i, t], {"dp": to})
-                    cp.start()
-                    sent.append(cp)
-                    self.given.append(cp)
+                    remote(xs[p].at[i, t], gx[p].at[i, dp], x_sem.at[p, 0],
+                           x_sem.at[p, 1], {"dp": to}).start()
 
         def open(self):
             part, p = self.part, self.p
-            for cp in self.given:
-                cp.wait_recv()
+            whole(xs[p].at[:, 1:ND], x_sem.at[p]).wait_recv()
             for i in range(2):
                 blk = block_at[(dp + 8 * i) % NS]
                 for t in range(ND):
@@ -343,64 +384,81 @@
             lax.fori_loop(0, 4, part, 0, unroll=True)
 
     class Train:
-        def __init__(self, part, way, towards, land, out, ascending):
-            self.part, self.p, self.land, self.out = part, part.p, land, out
-            self.ascending = ascending
+        def __init__(self, part, way, towards, refs, ascending):
+            self.part, self.p, self.ascending = part, part.p, ascending
+            self.near, self.far, self.later, self.one, self.zero, self.out2, self.out1 = refs
             self.line = Line(part.p, way, towards)
 
         def place(self, r):
             return r if self.ascending else NZ - r
 
-        def blocks(self, r, front, came):
-            p, part, out = self.p, self.part, self.out
+        def four(self):
+            some = slice(0, 2) if self.ascending else slice(2, 4)
+            self.line.go(0, ybuf[self.p][4].at[some], self.far)
+
+        def three(self):
+            self.line.go(1, ybuf[self.p][self.place(3)], self.near)
+
+        def three_far(self):
+            self.line.came(0)
+            self.line.go(2, self.far, self.later)
+
+        def code(self, r, j, part_rows, old):
             src = ((z + self.place(r)) % NZ) * NY + y
-            first, last, cut = (0, 4, part.front) if front else (4, NB, part.back)
+            o = plan[src * NB + j]
+            oz, oy = lax.shift_right_logical(o, 2), lax.bitwise_and(o, NY - 1)
+            new = ybuf[self.p][self.place(r)][oy][part_rows, :].astype(i32)
+            if r == 2:
+                before = (z + (NZ - 1 if self.ascending else 1)) % NZ
+                near = self.near[oy][part_rows, :].astype(i32)
+                far = self.later[lax.bitwise_and(o, 1)][part_rows, :].astype(i32)
+                at = jnp.full(near.shape, (oz == before).astype(i32), i32)
+                old = jnp.where(at > 0, near, far)
+            at = jnp.full(new.shape, (oz == z).astype(i32), i32)
+            return jnp.where(at > 0, new, old)
+
+        def blocks(self, r, first, last, out, came):
+            part = self.part
             for j in range(first, last):
                 rows = slice(j * part.rows, (j + 1) * part.rows)
-                o = plan[src * NB + j]
-                new = ybuf[p][self.place(r)][lax.rem(o, NY)][part.data, :]
-                if came is not None:
-                    at = jnp.full((part.rows, CH), (lax.div(o, NY) == z).astype(i32), i32)
-                    new = jnp.where(at > 0, new.astype(i32), came[rows, :].astype(i32)).astype(i16)
-                out[r - 1, rows, :] = new
-            return out.at[r - 1, cut], self.land[r - 1].at[cut]
-
-        def scales(self, r, came):
-            p, part, out = self.p, self.part, self.out
-            src = ((z + self.place(r)) % NZ) * NY + y
-            tile = jnp.zeros((16, CH), i32) if came is None else came[part.scales, :].astype(i32)
+                old = None if r == 2 else came[rows, :].astype(i32)
+                out[rows, :] = self.code(r, j, part.data, old).astype(i16)
+
+        def scales(self, r, out, came):
+            part = self.part
+            tile = jnp.zeros((16, CH), i32) if r == 2 else came[part.scales, :].astype(i32)
             for j in range(NB):
-                o = plan[src * NB + j]
-                new = ybuf[p][self.place(r)][lax.rem(o, NY)][part.tail, :].astype(i32)
-                at = (row_id // part.w == j).astype(i32) * (lax.div(o, NY) == z).astype(i32)
-                tile = jnp.where(at > 0, new, tile)
-            out[r - 1, part.scales, :] = tile.astype(i16)
-            return out.at[r - 1, part.scales], self.land[r - 1].at[part.scales]
-
-        def head(self, r):
-            came = None
-            if r < 3:
-                self.line.came(2 * (2 - r) + 1)
-                came = self.land[r]
-            self.line.go(2 * (3 - r) + 1, *self.blocks(r, not self.ascending, came))
-
-        def tail(self, r):
-            came = None
-            if r < 4:
-                self.line.came(2 * (2 - r) + 2, 10 - r)
-                came = self.land[r]
-            self.line.go(2 * (3 - r) + 2, *self.blocks(r, self.ascending, came))
-            self.line.go(11 - r, *self.scales(r, came))
+                new = self.code(r, j, part.tail, tile)
+                tile = jnp.where(row_id // part.w == j, new, tile)
+            out[part.scales, :] = tile.astype(i16)
+
+        def two(self):
+            part = self.part
+            self.line.came(1, 2)
+            self.blocks(2, 0, 4, self.out2, None)
+            self.line.go(3, self.out2.at[part.front], self.one.at[part.front])
+            self.blocks(2, 4, NB, self.out2, None)
+            self.scales(2, self.out2, None)
+            self.line.go(4, self.out2.at[part.rear], self.one.at[part.rear])
+
+        def last(self):
+            part = self.part
+            self.line.came(3)
+            self.blocks(1, 0, 4, self.out1, self.one)
+            self.line.go(5, self.out1.at[part.front], self.zero.at[part.front])
+            self.line.came(4)
+            self.blocks(1, 4, NB, self.out1, self.one)
+            self.scales(1, self.out1, self.one)
+            self.line.go(6, self.out1.at[part.rear], self.zero.at[part.rear])
 
         def arrived(self):
-            self.line.came(5, 6, 10)
+            self.line.came(5, 6)
 
     class Inward:
         def __init__(self, part):
             self.part, self.p = part, part.p
-            self.ups = Train(part, 2, up, ur[part.p], ush[part.p], True)
-            self.downs = Train(part, 3, down, dr[part.p], dsh[part.p], False)
-            self.hand, self.given = {}, []
+            self.ups = Train(part, 2, up, ur[part.p], True)
+            self.downs = Train(part, 3, down, dr[part.p], False)
 
         def multiply(self, i):
             part, p = self.part, self.p
@@ -427,34 +485,24 @@
             ux[p][dp + 8 * i] = xu[p][i, dp]
             for t in (4, 3, 5, 2, 6, 1, 7):
                 to = (dp + t) % ND
-                cp = remote(xu[p].at[i, to], ux[p].at[dp + 8 * i], x_sem.at[NP + p, 0, i, t],
-                            x_sem.at[NP + p, 1, i, t], {"dp": to})
-                cp.start()
-                sent.append(cp)
-                self.given.append(cp)
+                remote(xu[p].at[i, to], ux[p].at[dp + 8 * i], x_sem.at[NP + p, 0],
+                       x_sem.at[NP + p, 1], {"dp": to}).start()
 
         def arrive(self):
-            for cp in self.given:
-                cp.wait_recv()
+            whole(xu[self.p].at[:, 1:ND], x_sem.at[NP + self.p]).wait_recv()
 
         def across(self, n):
             p = self.p
             d = (z + n) % NZ
-            self.hand[n] = []
             for t in range(1, NY):
                 yy = (y + t) % NY
                 yback[p][n, t - 1] = ux[p][slot_of[d * NY + yy]]
-                cp = remote(yback[p].at[n, t - 1], ybuf[p][n].at[y],
-                            y_sem.at[NP + p, 0, n, t - 1], y_sem.at[NP + p, 1, n, t - 1],
-                            {"owner": z * NY + yy})
-                cp.start()
-                sent.append(cp)
-                self.hand[n].append(cp)
+                remote(yback[p].at[n, t - 1], ybuf[p][n].at[y], back_sem.at[p, n, 0],
+                       back_sem.at[p, n, 1], {"owner": z * NY + yy}).start()
             ybuf[p][n][y] = ux[p][slot_of[d * NY + y]]
 
         def crossed(self, n):
-            for cp in self.hand[n]:
-                cp.wait_recv()
+            whole(yback[self.p].at[n], back_sem.at[self.p, n]).wait_recv()
 
         def begin(self):
             self.across(4)
@@ -463,37 +511,33 @@
 
         def one(self):
             self.crossed(4)
-            self.ups.tail(4)
-            self.downs.tail(4)
+            self.ups.four()
+            self.downs.four()
             self.crossed(3)
-            self.ups.head(3)
+            self.ups.three()
             self.crossed(5)
-            self.downs.head(3)
+            self.downs.three()
             self.across(2)
             self.across(6)
 
         def two(self):
-            self.ups.tail(3)
-            self.downs.tail(3)
+            self.ups.three_far()
+            self.downs.three_far()
             self.across(1)
             self.across(7)
+
+        def three(self):
             self.crossed(2)
-            self.ups.head(2)
+            self.ups.two()
             self.crossed(6)
-            self.downs.head(2)
-
-        def three(self):
-            self.ups.tail(2)
-            self.downs.tail(2)
+            self.downs.two()
             self.across(0)
+
+        def four(self):
             self.crossed(1)
-            self.ups.head(1)
+            self.ups.last()
             self.crossed(7)
-            self.downs.head(1)
-
-        def four(self):
-            self.ups.tail(1)
-            self.downs.tail(1)
+            self.downs.last()
 
         def finish(self):
             part, p = self.part, self.p
@@ -502,27 +546,24 @@
             self.downs.arrived()
             for j in range(NB):
                 o = plan[me * NB + j]
-                near = ybuf[p][0][lax.rem(o, NY)].astype(i32)
-                off = lax.rem(lax.div(o, NY) + NZ - z, NZ)
-                above = (off < 4).astype(i32)
-                if j >= 4:
-                    above = above + (off == 4).astype(i32)
+                near = ybuf[p][0][lax.bitwise_and(o, NY - 1)].astype(i32)
+                off = lax.bitwise_and(lax.shift_right_logical(o, 2) + NZ - z, NZ - 1)
+                above = jnp.where(off < 4, 1, jnp.where(
+                    off == 4, lax.shift_right_logical(lax.bitwise_and(o, NY - 1), 1), 0))
                 local = (off == 0).astype(i32)
                 rows = slice(j * part.rows, (j + 1) * part.rows)
                 full = jnp.zeros((part.rows, CH), i32)
-                code = jnp.where(full + above > 0, dr[p][0][rows, :].astype(i32),
-                                 ur[p][0][rows, :].astype(i32))
+                code = jnp.where(full + above > 0, dr[p][4][rows, :].astype(i32),
+                                 ur[p][4][rows, :].astype(i32))
                 code = jnp.where(full + local > 0, near[part.data, :], code)
-                tile = jnp.where(row_id * 0 + above > 0, dr[p][0][part.scales, :].astype(i32),
-                                 ur[p][0][part.scales, :].astype(i32))
+                tile = jnp.where(row_id * 0 + above > 0, dr[p][4][part.scales, :].astype(i32),
+                                 ur[p][4][part.scales, :].astype(i32))
                 tile = jnp.where(row_id * 0 + local > 0, near[part.tail, :], tile)
                 tile = scale_of(tile)
                 for kk, n in enumerate(part.chunks):
                     r = j * part.w + kk
                     update[j, :, n * CH:n * CH + CH] = (
                         code[kk * SR:kk * SR + SR].astype(f32) * tile[r:r + 1, :])
-
-    stat_came = [[], []]
 
     def stat(which, i):
         def block(m, _):
@@ -548,15 +589,11 @@
         sr[which][dp + 8 * i] = sx[which][i, dp]
         for t in (4, 3, 5, 2, 6, 1, 7):
             to = (dp + t) % ND
-            cp = remote(sx[which].at[i, to], sr[which].at[dp + 8 * i], x_sem.at[2 * NP + which, 0, i, t],
-                        x_sem.at[2 * NP + which, 1, i, t], {"dp": to})
-            cp.start()
-            sent.append(cp)
-            stat_came[which].append(cp)
+            remote(sx[which].at[i, to], sr[which].at[dp + 8 * i], x_sem.at[2 * NP + which, 0],
+                   x_sem.at[2 * NP + which, 1], {"dp": to}).start()
 
     def renew(which, held, out):
-        for cp in stat_came[which]:
-            cp.wait_recv()
+        whole(sx[which].at[:, 1:ND], x_sem.at[2 * NP + which]).wait_recv()
 
         def slot(k, _):
             w = weight[k]
@@ -565,7 +602,7 @@
                 cols = slice(n * CH, n * CH + CH)
                 term = widen(sr[which][k, n * SR:n * SR + SR, :]) * scales[n:n + 1, :]
                 held[k, :, cols] = stat_decay * held[k, :, cols] + w * term
-            pltpu.make_async_copy(held.at[k], out.at[k], out_sem.at[which, k]).start()
+            pltpu.make_async_copy(held.at[k], out.at[k], out_sem.at[which]).start()
             return 0
 
         lax.fori_loop(0, NS, slot, 0)
@@ -631,17 +668,13 @@
     out1.start()
     out0.step(2)
     total(PARTS[2])
-    roots = []
     for which, (src, dst) in enumerate(((left_root, lf), (right_root, rf))):
         for i in range(2):
             for t in range(1, ND):
                 to = (dp + t) % ND
-                cp = remote(src.at[(to + 8 * i) % NS], dst.at[i, rows_of(dp)],
-                            x_sem.at[2 * NP + 2 + which, 0, i, t],
-                            x_sem.at[2 * NP + 2 + which, 1, i, t], {"dp": to})
-                cp.start()
-                sent.append(cp)
-                roots.append(cp)
+                remote(src.at[(to + 8 * i) % NS], dst.at[i, rows_of(dp)],
+                       x_sem.at[2 * NP + 2 + which, 0],
+                       x_sem.at[2 * NP + 2 + which, 1], {"dp": to}).start()
     out0.step(3)
     out1.step(1)
     place_slots()
@@ -657,8 +690,8 @@
     out2.step(2)
     for cp in root_in:
         cp.wait()
-    for cp in roots:
-        cp.wait_recv()
+    whole(lf.at[:, 0:7 * SR], x_sem.at[2 * NP + 2]).wait_recv()
+    whole(rf.at[:, 0:7 * SR], x_sem.at[2 * NP + 3]).wait_recv()
     out0.project()
     out2.step(3)
     out1.open()
@@ -709,13 +742,9 @@
     renew(1, rs, right_new)
     in2.finish()
 
-    def done(k, _):
-        pltpu.make_async_copy(ls.at[k], left_new.at[k], out_sem.at[0, k]).wait()
-        pltpu.make_async_copy(rs.at[k], right_new.at[k], out_sem.at[1, k]).wait()
-        return 0
-
-    lax.fori_loop(0, NS, done, 0)
-    for cp in sent:
+    pltpu.make_async_copy(ls, left_new, out_sem.at[0]).wait()
+    pltpu.make_async_copy(rs, right_new, out_sem.at[1]).wait()
+    for cp in sent + group:
         cp.wait_send()
 
 
@@ -731,6 +760,10 @@
 
     def message(part):
         return part.message
+
+    train = [vmem(shape, i16) for part in PARTS for shape in (
+        (NY, part.message, CH), (2, part.message, CH), (2, part.message, CH),
+        *[(part.unit, CH)] * 4)]
 
     return pl.pallas_call(
         shampoo_kernel,
@@ -751,7 +784,8 @@
             vmem((12, UNIT, CH), i16),
             vmem((12, UNIT, CH), i16),
             *each((), unit),
-            *each((), unit, 7),
+            *[vmem((rows, CH), i16) for part in PARTS for rows in (
+                *[part.unit] * 4, part.six, part.six, 2 * part.far, part.six, part.six)],
             *each((NZ, NY - 1), message),
             *each((NO,), message),
             *each((2, ND), message),
@@ -761,10 +795,8 @@
             *each((2 * ND,), message),
             *each((NY,), message, NZ),
             *each((NZ, NY - 1), message),
-            *each((), unit, 4),
-            *each((), unit, 4),
-            *each((4,), unit),
-            *each((4,), unit),
+            *train,
+            *train,
             *[vmem((2, ND, SLOT, CH), i16)] * 2,
             *[vmem((2 * ND, SLOT, CH), i16)] * 2,
             vmem((NS, SR, BO), f32),
@@ -773,10 +805,11 @@
             pltpu.SemaphoreType.DMA((2, 4)),
             pltpu.SemaphoreType.DMA((10,)),
             pltpu.SemaphoreType.DMA((2, 12)),
-            pltpu.SemaphoreType.DMA((NP, 4, 2, 11)),
-            pltpu.SemaphoreType.DMA((2 * NP, 2, NZ, NY - 1)),
-            pltpu.SemaphoreType.DMA((2 * NP + 4, 2, 2, ND)),
-            pltpu.SemaphoreType.DMA((2, NS)),
+            pltpu.SemaphoreType.DMA((NP, 4, 2, 7)),
+            pltpu.SemaphoreType.DMA((NP, 2)),
+            pltpu.SemaphoreType.DMA((NP, NZ, 2)),
+            pltpu.SemaphoreType.DMA((2 * NP + 4, 2)),
+            pltpu.SemaphoreType.DMA((2,)),
         ],
         compiler_params=pltpu.CompilerParams(
             collective_id=0, has_side_effects=True, vmem_limit_bytes=LIMIT),

time: 154 us -> 149 us (0.968)
  Pallas kernels: 146 us -> 142 us
    pallas_call x1, Pallas kernels: 146 us -> 142 us  [shampoo(): pl.pallas_call(shampoo_kernel, out_shape=(jax.ShapeDtypeStruct((NS, SR, B...]
where the time goes in v5:
time: 149 us; the launch traced here: 148 us
  Pallas kernels  142 us (95%)
  local copies, waits for them, and re-layouts  5.62 us (4%)
    pallas_call x1, Pallas kernels, shampoo(): pl.pallas_call(shampoo_kernel, out_shape=(jax.ShapeDtypeStruct((NS, SR, B...  142 us
    unnamed x7, local copies, waits for them, and re-layouts  5.62 us

profile of v5, /device:TPU:8, one launch (start us, length us, event | category | flops | bytes accessed | tf_op | source)
XLA Modules:
  0.0 148.2 jit_solution(4075300850261303789)
XLA Ops:
  0.6 141.9 %shampoo.1 = (f32[13,64,512]{2,1,0:T(8,128)}, f32[13,64,512]{2,1,0:T(8,128)}, f32[7,64,512]{2,1,0:T(8,128)}) custom-call(s32[224]{0:T(256)} %plan.1, bf16[7,512,512]{2,1,0:T(8,128)(2,1)} %bitcast.7, f32[13,64,512]{2,1,0:T(8,128)} %bitcast.8, f32[13,64,512]{2,1,0:T(8,128)} %bitcast.9, bf16[13,64,512]{2,1,0:T(8,128)(2,1)} %bitcast.12, ...), custom_call_target="tpu_custom_call" | custom-call | tf_op jit(solution)/shard_map/shampoo/pallas_call | solution.py:768
  142.6 0.0 copy-start
  142.6 2.9 %copy.12 = f32[1,13,64,512]{3,2,1,0:T(8,128)} copy(f32[1,13,64,512]{3,2,1,0:T(8,128)} %bitcast.11) | data formatting | bytes 3407872
  145.5 0.0 copy-done
  145.5 0.0 copy-start.1
  145.5 1.2 copy.13
  146.7 0.6 copy-done.1
  147.3 0.9 copy.14
Async XLA Ops:
  142.6 2.9 %copy-start = (f32[13,64,512]{2,1,0:T(8,128)S(1)}, f32[13,64,512]{2,1,0:T(8,128)}, u32[]{:S(2)}) copy-start(f32[13,64,512]{2,1,0:T(8,128)} %get-tuple-element.7) | copy-start | bytes 5111812
  145.5 1.8 %copy-start.1 = (f32[7,64,512]{2,1,0:T(8,128)S(1)}, f32[7,64,512]{2,1,0:T(8,128)}, u32[]{:S(2)}) copy-start(f32[7,64,512]{2,1,0:T(8,128)} %get-tuple-element.14) | copy-start | bytes 2752516

commit v6 on v5

--- a/solution.py
+++ b/solution.py
@@ -73,7 +73,7 @@
         self.six = 6 * SR * w + 16
 
 
-PARTS = (Part(0, (0,)), Part(1, (1, 2)), Part(2, (3,)))
+PARTS = (Part(0, (0, 1)), Part(1, (2, 3)))
 NP = len(PARTS)
 
 
@@ -151,10 +151,8 @@
         t = ((x + off) % 4) * 2 + 1 - c
         pair[n] = remote(grads.at[:, rows_of(t), :], par.at[n],
                          pair_sem.at[0, n], pair_sem.at[1, n], {"dp": partner})
-        pair[n].start()
         sent.append(pair[n])
-    for cp in root_in + stat_in:
-        cp.start()
+    pair[0].start()
 
     def stand(i, count):
         hold, which = jnp.int32(0), jnp.int32(0)
@@ -607,19 +605,19 @@
 
         lax.fori_loop(0, NS, slot, 0)
 
-    out0, out1, out2 = (Outward(part) for part in PARTS)
-    in0, in1, in2 = (Inward(part) for part in PARTS)
+    out0, out1 = (Outward(part) for part in PARTS)
+    in0, in1 = (Inward(part) for part in PARTS)
     right_far, left_far, right_straight, left_straight, right_both, left_both = {}, {}, {}, {}, {}, {}
 
     def far(k):
         fill(snd.at[k], 1, lambda j, kk: pair_sum(0, j, k))
-        if k < 2:
+        if k % 2 == 0:
             right_far[k] = ship(k, right)
         else:
             left_far[k] = ship(k, left)
 
     def straight(k):
-        if k >= 2:
+        if k % 2 == 1:
             fill(snd.at[4 + k], 1, lambda j, kk: pair_sum(1, j, k))
             right_straight[k] = ship(4 + k, right)
         else:
@@ -627,7 +625,7 @@
             left_straight[k] = ship(4 + k, left)
 
     def both(k):
-        if k < 2:
+        if k % 2 == 0:
             right_far[k].wait_recv()
             fill(snd.at[8 + k], 1, lambda j, kk: pair_sum(1, j, k) + received(k, j))
             right_both[k] = ship(8 + k, right)
@@ -646,16 +644,21 @@
             + received(8 + part.chunks[kk], j)))
 
     ready(0)
+    pair[2].start()
+    pair[1].start()
+    pair[3].start()
+    for cp in root_in + stat_in:
+        cp.start()
     far(0)
     far(1)
     ready(2)
     straight(0)
+    ready(1)
+    straight(1)
+    both(0)
+    both(1)
     far(2)
     far(3)
-    ready(1)
-    both(0)
-    straight(1)
-    both(1)
     straight(2)
     straight(3)
     ready(3)
@@ -663,11 +666,7 @@
     out0.start()
     both(2)
     both(3)
-    out0.step(1)
     total(PARTS[1])
-    out1.start()
-    out0.step(2)
-    total(PARTS[2])
     for which, (src, dst) in enumerate(((left_root, lf), (right_root, rf))):
         for i in range(2):
             for t in range(1, ND):
@@ -675,31 +674,26 @@
                 remote(src.at[(to + 8 * i) % NS], dst.at[i, rows_of(dp)],
                        x_sem.at[2 * NP + 2 + which, 0],
                        x_sem.at[2 * NP + 2 + which, 1], {"dp": to}).start()
+    out0.step(1)
+    place_slots()
+    out0.step(2)
     out0.step(3)
+    out1.start()
+    out0.last()
     out1.step(1)
-    place_slots()
-    out0.last()
+    out0.spread()
     out1.step(2)
-    out0.spread()
+    out0.open()
     out1.step(3)
-    out2.start()
-    out0.open()
-    out1.last()
-    out2.step(1)
-    out1.spread()
-    out2.step(2)
     for cp in root_in:
         cp.wait()
     whole(lf.at[:, 0:7 * SR], x_sem.at[2 * NP + 2]).wait_recv()
     whole(rf.at[:, 0:7 * SR], x_sem.at[2 * NP + 3]).wait_recv()
     out0.project()
-    out2.step(3)
+    out1.last()
+    out1.spread()
     out1.open()
     out1.project()
-    out2.last()
-    out2.spread()
-    out2.open()
-    out2.project()
     in0.multiply(0)
     in0.hand_out(0)
     in0.multiply(1)
@@ -708,39 +702,28 @@
     in1.multiply(1)
     in0.arrive()
     in0.begin()
+    in0.one()
     in1.hand_out(0)
     in1.hand_out(1)
-    in0.one()
-    in2.multiply(0)
-    in2.multiply(1)
     in0.two()
+    stat(0, 0)
+    in0.three()
     in1.arrive()
     in1.begin()
-    in2.hand_out(0)
-    in2.hand_out(1)
+    stat(1, 0)
+    in0.four()
     in1.one()
-    in0.three()
-    stat(0, 0)
-    in0.four()
+    stat(0, 1)
+    in0.finish()
     in1.two()
-    stat(1, 0)
-    in2.arrive()
-    in2.begin()
+    stat(1, 1)
     in1.three()
-    in2.one()
-    stat(0, 1)
-    in1.four()
-    in0.finish()
-    in2.two()
-    stat(1, 1)
-    in2.three()
     for cp in stat_in:
         cp.wait()
+    renew(0, ls, left_new)
+    in1.four()
+    renew(1, rs, right_new)
     in1.finish()
-    in2.four()
-    renew(0, ls, left_new)
-    renew(1, rs, right_new)
-    in2.finish()
 
     pltpu.make_async_copy(ls, left_new, out_sem.at[0]).wait()
     pltpu.make_async_copy(rs, right_new, out_sem.at[1]).wait()

time: 149 us -> 140 us (0.940)
  Pallas kernels: 142 us -> 133 us
    pallas_call x1, Pallas kernels: 142 us -> 133 us  [shampoo(): pl.pallas_call(shampoo_kernel, out_shape=(jax.ShapeDtypeStruct((NS, SR, B...]
where the time goes in v6:
time: 140 us; the launch traced here: 139 us
  Pallas kernels  133 us (95%)
  local copies, waits for them, and re-layouts  5.62 us (4%)
    pallas_call x1, Pallas kernels, shampoo(): pl.pallas_call(shampoo_kernel, out_shape=(jax.ShapeDtypeStruct((NS, SR, B...  133 us
    unnamed x7, local copies, waits for them, and re-layouts  5.62 us

profile of v6, /device:TPU:8, one launch (start us, length us, event | category | flops | bytes accessed | tf_op | source)
XLA Modules:
  0.0 139.1 jit_solution(4689843614719117561)
XLA Ops:
  0.6 132.8 %shampoo.1 = (f32[13,64,512]{2,1,0:T(8,128)}, f32[13,64,512]{2,1,0:T(8,128)}, f32[7,64,512]{2,1,0:T(8,128)}) custom-call(s32[224]{0:T(256)} %plan.1, bf16[7,512,512]{2,1,0:T(8,128)(2,1)} %bitcast.7, f32[13,64,512]{2,1,0:T(8,128)} %bitcast.8, f32[13,64,512]{2,1,0:T(8,128)} %bitcast.9, bf16[13,64,512]{2,1,0:T(8,128)(2,1)} %bitcast.12, ...), custom_call_target="tpu_custom_call" | custom-call | tf_op jit(solution)/shard_map/shampoo/pallas_call | solution.py:751
  133.5 0.0 copy-start
  133.5 2.9 %copy.12 = f32[1,13,64,512]{3,2,1,0:T(8,128)} copy(f32[1,13,64,512]{3,2,1,0:T(8,128)} %bitcast.11) | data formatting | bytes 3407872
  136.4 0.0 copy-done
  136.4 0.0 copy-start.1
  136.4 1.2 copy.13
  137.6 0.6 copy-done.1
  138.2 0.9 copy.14
Async XLA Ops:
  133.5 2.9 %copy-start = (f32[13,64,512]{2,1,0:T(8,128)S(1)}, f32[13,64,512]{2,1,0:T(8,128)}, u32[]{:S(2)}) copy-start(f32[13,64,512]{2,1,0:T(8,128)} %get-tuple-element.7) | copy-start | bytes 5111812
  136.4 1.8 %copy-start.1 = (f32[7,64,512]{2,1,0:T(8,128)S(1)}, f32[7,64,512]{2,1,0:T(8,128)}, u32[]{:S(2)}) copy-start(f32[7,64,512]{2,1,0:T(8,128)} %get-tuple-element.14) | copy-start | bytes 2752516

commit v7 on v6

--- a/solution.py
+++ b/solution.py
@@ -354,32 +354,33 @@
                     remote(xs[p].at[i, t], gx[p].at[i, dp], x_sem.at[p, 0],
                            x_sem.at[p, 1], {"dp": to}).start()
 
-        def open(self):
+        def arrive(self):
+            whole(xs[self.p].at[:, 1:ND], x_sem.at[self.p]).wait_recv()
+
+        def open(self, i):
             part, p = self.part, self.p
-            whole(xs[p].at[:, 1:ND], x_sem.at[p]).wait_recv()
-            for i in range(2):
-                blk = block_at[(dp + 8 * i) % NS]
-                for t in range(ND):
-                    scales = scale_of(gx[p][i, t, part.tail, :])
-                    for kk, n in enumerate(part.chunks):
-                        v = (widen(gx[p][i, t, kk * SR:kk * SR + SR, :])
-                             * scale_row(scales, blk * part.w + kk))
-                        hi, lo = split(v)
-                        ghi[i, t * SR:t * SR + SR, n * CH:n * CH + CH] = hi
-                        glo[i, t * SR:t * SR + SR, n * CH:n * CH + CH] = lo
-
-        def project(self):
+            blk = block_at[(dp + 8 * i) % NS]
+            for t in range(ND):
+                scales = scale_of(gx[p][i, t, part.tail, :])
+                for kk, n in enumerate(part.chunks):
+                    v = (widen(gx[p][i, t, kk * SR:kk * SR + SR, :])
+                         * scale_row(scales, blk * part.w + kk))
+                    hi, lo = split(v)
+                    ghi[i, t * SR:t * SR + SR, n * CH:n * CH + CH] = hi
+                    glo[i, t * SR:t * SR + SR, n * CH:n * CH + CH] = lo
+
+        def project(self, i):
             cols = self.part.cols
 
             def part(m, _):
-                i, rows = m // 2, rows_of(m % 2, 256)
+                rows = rows_of(m, 256)
                 p = dot(lf[i, rows, :], ghi[i, :, cols]) + dot(lf[i, rows, :], glo[i, :, cols])
                 hi, lo = split(p)
                 phi[i, rows, cols] = hi
                 plo[i, rows, cols] = lo
                 return 0
 
-            lax.fori_loop(0, 4, part, 0, unroll=True)
+            lax.fori_loop(0, 2, part, 0, unroll=True)
 
     class Train:
         def __init__(self, part, way, towards, refs, ascending):
@@ -584,6 +585,8 @@
             return 0
 
         lax.fori_loop(0, 4, block, 0, unroll=2)
+
+    def give(which, i):
         sr[which][dp + 8 * i] = sx[which][i, dp]
         for t in (4, 3, 5, 2, 6, 1, 7):
             to = (dp + t) % ND
@@ -666,6 +669,7 @@
     out0.start()
     both(2)
     both(3)
+    out0.step(1)
     total(PARTS[1])
     for which, (src, dst) in enumerate(((left_root, lf), (right_root, rf))):
         for i in range(2):
@@ -674,7 +678,6 @@
                 remote(src.at[(to + 8 * i) % NS], dst.at[i, rows_of(dp)],
                        x_sem.at[2 * NP + 2 + which, 0],
                        x_sem.at[2 * NP + 2 + which, 1], {"dp": to}).start()
-    out0.step(1)
     place_slots()
     out0.step(2)
     out0.step(3)
@@ -683,40 +686,50 @@
     out1.step(1)
     out0.spread()
     out1.step(2)
-    out0.open()
+    out0.arrive()
+    out0.open(0)
+    out0.open(1)
     out1.step(3)
+    out1.last()
+    out1.spread()
     for cp in root_in:
         cp.wait()
     whole(lf.at[:, 0:7 * SR], x_sem.at[2 * NP + 2]).wait_recv()
     whole(rf.at[:, 0:7 * SR], x_sem.at[2 * NP + 3]).wait_recv()
-    out0.project()
-    out1.last()
-    out1.spread()
-    out1.open()
-    out1.project()
+    out0.project(0)
+    out0.project(1)
+    out1.arrive()
+    out1.open(0)
+    out1.project(0)
     in0.multiply(0)
     in0.hand_out(0)
+    out1.open(1)
+    out1.project(1)
     in0.multiply(1)
     in0.hand_out(1)
     in1.multiply(0)
     in1.multiply(1)
+    stat(0, 0)
     in0.arrive()
     in0.begin()
     in0.one()
     in1.hand_out(0)
     in1.hand_out(1)
+    give(0, 0)
     in0.two()
-    stat(0, 0)
+    stat(1, 0)
+    give(1, 0)
     in0.three()
     in1.arrive()
     in1.begin()
-    stat(1, 0)
     in0.four()
     in1.one()
     stat(0, 1)
+    give(0, 1)
     in0.finish()
+    stat(1, 1)
+    give(1, 1)
     in1.two()
-    stat(1, 1)
     in1.three()
     for cp in stat_in:
         cp.wait()

time: 140 us -> 140 us (level)
  no operation moved by 1% of the time
where the time goes in v7:
time: 140 us
  Pallas kernels  134 us (96%)
  local copies, waits for them, and re-layouts  5.62 us (4%)
    pallas_call x1, Pallas kernels, shampoo(): pl.pallas_call(shampoo_kernel, out_shape=(jax.ShapeDtypeStruct((NS, SR, B...  134 us
    unnamed x7, local copies, waits for them, and re-layouts  5.62 us

profile of v7, /device:TPU:8, one launch (start us, length us, event | category | flops | bytes accessed | tf_op | source)
XLA Modules:
  0.0 140.1 jit_solution(4068740131603690253)
XLA Ops:
  0.6 133.8 %shampoo.1 = (f32[13,64,512]{2,1,0:T(8,128)}, f32[13,64,512]{2,1,0:T(8,128)}, f32[7,64,512]{2,1,0:T(8,128)}) custom-call(s32[224]{0:T(256)} %plan.1, bf16[7,512,512]{2,1,0:T(8,128)(2,1)} %bitcast.7, f32[13,64,512]{2,1,0:T(8,128)} %bitcast.8, f32[13,64,512]{2,1,0:T(8,128)} %bitcast.9, bf16[13,64,512]{2,1,0:T(8,128)(2,1)} %bitcast.12, ...), custom_call_target="tpu_custom_call" | custom-call | tf_op jit(solution)/shard_map/shampoo/pallas_call | solution.py:764
  134.5 0.0 copy-start
  134.5 2.9 %copy.12 = f32[1,13,64,512]{3,2,1,0:T(8,128)} copy(f32[1,13,64,512]{3,2,1,0:T(8,128)} %bitcast.11) | data formatting | bytes 3407872
  137.4 0.0 copy-done
  137.4 0.0 copy-start.1
  137.4 1.2 copy.13
  138.6 0.6 copy-done.1
  139.2 0.9 copy.14
Async XLA Ops:
  134.5 2.9 %copy-start = (f32[13,64,512]{2,1,0:T(8,128)S(1)}, f32[13,64,512]{2,1,0:T(8,128)}, u32[]{:S(2)}) copy-start(f32[13,64,512]{2,1,0:T(8,128)} %get-tuple-element.7) | copy-start | bytes 5111812
  137.4 1.8 %copy-start.1 = (f32[7,64,512]{2,1,0:T(8,128)S(1)}, f32[7,64,512]{2,1,0:T(8,128)}, u32[]{:S(2)}) copy-start(f32[7,64,512]{2,1,0:T(8,128)} %get-tuple-element.14) | copy-start | bytes 2752516
